TPU v7x, 32 devices: a whole 2x2x4 slice. The times are simulated.
32 devices in a mesh: jpair: 2 (over x), blk: 16 (over z, y, core).
Axes of the slice: x: 2, y: 2, z: 4, core: 2. Of those that a mesh axis runs over, the one named last changes fastest.
Arguments:
- dipole: bfloat16 [256, 12, 3, 256, 256], P('blk'), may hold values from -24 to 24
- block_cols: int32 [256, 12], P('blk'), may hold values from 0 to 255, as said below
- upper_vecs: bfloat16 [131072, 256], P(('jpair', 'blk')), parts along dimension 0, may hold values from -0.0234375 to 0.0234375
- lower_vecs: bfloat16 [131072, 128], P(('jpair', 'blk')), parts along dimension 0, may hold values from -0.0234375 to 0.0234375
- upper_energy: float32 [512], P('jpair'), parts along dimension 0, may hold values from 1 to 2
- lower_energy: float32 [256], P('jpair'), parts along dimension 0, may hold values from 0 to 0.8
Outputs:
- strength: float32 [512, 128], P(('jpair', 'blk')), parts along dimension 0
- intensity: float32 [512, 128], P(('jpair', 'blk')), parts along dimension 0
There are 2 independent parts, one for each index of `jpair`. A program takes and returns all parts, laid end to end along the dimension named above; an argument that names none is the same for every part. Nothing has to cross between parts.
Inputs may be any that keep to these rules, and one draw needn't show every extreme that they name: `block_cols`: within one block row the 12 block columns are distinct, and one of them is the row's own index. Splitting the block rows into 16 equal runs of consecutive rows, the columns of one run that fall in another run number at most 12 distinct blocks for each other run, and exactly 12 for some.
All inputs are finite; a program needn't handle non-finite values.
Results may differ from a plain program's by a relative error of at most 0.0026.
Values may be sent and summed in bfloat16 or wider, within the bound.
No kernel may reach another device: no remote copies, remote signals or barrier semaphores. Data moves between devices by JAX's collectives and lax.ppermute only.
A program may use at most 256 MiB of HBM per device.

v0:
```python
import jax
import jax.numpy as jnp
from jax import lax
from jax.sharding import PartitionSpec as P

THERMAL = 0.3


def per_device(dipole, block_cols, upper_vecs, lower_vecs, upper_energy, lower_energy):
    rows_blk, nonzero, n_comps, block_size, _ = dipole.shape
    upper_count = upper_vecs.shape[1]
    lower_count = lower_vecs.shape[1]
    upper_blocks = upper_vecs.reshape(rows_blk, block_size, upper_count)
    halves = jnp.einsum(
        "rkast,rsu->rkatu", dipole, upper_blocks, preferred_element_type=jnp.float32
    ).astype(jnp.bfloat16)
    entry_count = rows_blk * nonzero
    halves = halves.reshape(entry_count, n_comps, block_size, upper_count)
    columns = block_cols.reshape(entry_count)
    group_size = lax.axis_size("blk")
    my_index = lax.axis_index("blk")
    gathered = lax.all_gather(lower_vecs, "blk", axis=0, tiled=True)
    all_blocks = gathered.reshape(gathered.shape[0] // block_size, block_size, lower_count)
    lows = jnp.take(all_blocks, columns, axis=0)
    proj = jnp.einsum("eatu,etl->aul", halves, lows, preferred_element_type=jnp.float32)
    share_rows = upper_count // group_size
    first_row = my_index * share_rows
    summed = lax.psum(proj, "blk")
    own_share = lax.dynamic_slice_in_dim(summed, first_row, share_rows, 1)
    strength = jnp.sum(own_share * own_share, axis=0)
    energy_rows = lax.dynamic_slice_in_dim(upper_energy, first_row, share_rows, 0)
    wavenumber = energy_rows[:, None] - lower_energy[None, :]
    intensity = wavenumber**3 * jnp.exp(-lower_energy / THERMAL)[None, :] * strength
    return (strength, intensity)


def solution(mesh):
    placed = (
        P("blk", None, None, None, None),
        P("blk", None),
        P(("jpair", "blk"), None),
        P(("jpair", "blk"), None),
        P("jpair"),
        P("jpair"),
    )
    return jax.shard_map(
        per_device,
        mesh=mesh,
        in_specs=placed,
        out_specs=(P(("jpair", "blk"), None), P(("jpair", "blk"), None)),
        check_vma=False,
    )
```

profile of v0, /device:TPU:0, one launch (start us, length us, event | category | flops | bytes accessed | tf_op | source)
XLA Modules:
  0.0 283.5 jit_solution(16496702931421474902)
XLA Ops:
  7.2 0.0 copy-start
  7.2 0.0 all-gather.2.cloned.1.call-start
  7.2 0.7 all-gather.2.cloned.1.call-update
  7.9 0.0 all-reduce.2.cloned.1.call-start
  8.0 0.8 reshape.59
  8.8 0.8 reshape.57
  9.5 0.8 dynamic_slice.7
  10.3 0.0 copy-done
  10.3 59.0 %convolution_convert_fusion = bf16[16,12,3,256,256]{4,3,2,1,0:T(8,128)(2,1)} fusion(bf16[16,12,3,256,256]{4,3,2,1,0:T(8,128)(2,1)} %param.6, bf16[16,256,256,1,1]{2,1,4,3,0:T(8,128)(2,1)S(1)} %bitcast.20), kind=kOutput, calls=%fused_computation.1 | convolution fusion | flops 19365101568 | bytes 153092096 | tf_op jit(solution)/shard_map/rkast,rsu->rkatu/dot_general | solution.py:14
  69.4 70.4 %all-gather.2.cloned.1.call-done = bf16[65536,128]{1,0:T(8,128)(2,1)} async-done(((bf16[4096,128]{1,0:T(8,128)(2,1)}), bf16[65536,128]{1,0:T(8,128)(2,1)}) %all-gather.2.cloned.1.call-update) | async-done | bytes 16777232 | tf_op jit(solution)/shard_map/all_gather | solution.py:22
  139.8 13.9 %gather_fusion = bf16[192,256,128]{2,1,0:T(8,128)(2,1)} fusion(bf16[256,256,128]{2,1,0:T(8,128)(2,1)} %bitcast.21, s32[1024]{0:T(1024)S(1)} %pad_clamp_fusion), kind=kCustom, calls=%fused_computation | custom fusion | bytes 25166592 | tf_op jit(solution)/shard_map/jit(_take)/gather | solution.py:24
  153.7 0.0 copy-start.2
  153.8 32.8 %fusion.5 = f32[3,256,128]{2,1,0:T(8,128)} fusion(bf16[192,3,256,256]{3,2,1,0:T(8,128)(2,1)} %bitcast.3, bf16[192,256,128]{2,1,0:T(8,128)(2,1)} %gather_fusion, pred[192]{0:T(512)(128)(4,1)S(1)} %compare_and_fusion), kind=kOutput, calls=%fused_computation.7 | convolution fusion | flops 9669967872 | bytes 88473792 | tf_op jit(solution)/shard_map/eatu,etl->aul/dot_general | solution.py:25
  186.6 0.0 all-reduce.2.cloned.1.call-update
  186.6 0.0 copy-done.2
  186.6 88.6 %all-reduce.2.cloned.1.call-done = f32[3,256,128]{2,1,0:T(8,128)} async-done(((f32[3,256,128]{2,1,0:T(8,128)}), f32[3,256,128]{2,1,0:T(8,128)}) %all-reduce.2.cloned.1.call-update) | async-done | bytes 393232 | tf_op jit(solution)/shard_map/psum | solution.py:28
  275.2 0.7 multiply_reduce_fusion
  276.0 0.0 copy-start.1
  276.0 0.7 fusion.9
  276.7 0.0 copy-done.1
  (4 shorter events, 0.0 us)
Async XLA Ops:
  7.2 3.2 %copy-start = (bf16[4096,256]{1,0:T(8,128)(2,1)S(1)}, bf16[4096,256]{1,0:T(8,128)(2,1)}, u32[]{:S(2)}) copy-start(bf16[4096,256]{1,0:T(8,128)(2,1)} %param.8) | copy-start | bytes 6291460
  7.2 132.6 %all-gather.2.cloned.1.call-start = ((), (), s32[]{:S(2)}) async-start(), calls=%async_computation | async-start | bytes 17825792 | tf_op jit(solution)/shard_map/all_gather | solution.py:22
  7.9 267.3 %all-reduce.2.cloned.1.call-start = ((), (), s32[]{:S(2)}) async-start(), calls=%async_computation.1 | async-start | bytes 786432 | tf_op jit(solution)/shard_map/psum | solution.py:28
  153.7 32.8 %copy-start.2 = (f32[128]{0:T(128)S(1)}, f32[128]{0:T(128)}, u32[]{:S(2)}) copy-start(f32[128]{0:T(128)} %param.11) | copy-start | bytes 1540
  276.0 0.7 copy-start.1
Sparse Core Ops, SparseCore 0:
  10.2 129.5 all-gather.1
  186.7 88.4 all-reduce.1
where the time goes:
time: 284 us; the launch traced here: 283 us
  waiting for transfers between devices  160 us (56%)
  matrix products  91.9 us (32%)
  local copies, waits for them, and re-layouts  16.3 us (6%)
  between operations  14.1 us (5%)
    psum x1, waiting for transfers between devices, per_device(): summed = lax.psum(proj, 'blk')  88.6 us
    all_gather x1, waiting for transfers between devices, per_device(): gathered = lax.all_gather(lower_vecs, 'blk', axis=0, tiled=True)  70.4 us
    dot_general x1, matrix products, per_device(): jnp.einsum('rkast,rsu->rkatu', dipole, upper_blocks, preferred_element_ty...  59 us
    dot_general x1, matrix products, per_device(): jnp.einsum('eatu,etl->aul', halves, lows, preferred_element_type=jnp.floa...  32.8 us
    gather x1, local copies, waits for them, and re-layouts, per_device(): lows = jnp.take(all_blocks, columns, axis=0)  13.9 us
  transfers between devices with their start and end apart: 2, of which 2 were waited for; matrix products, arithmetic and copies ran while one was open for 22% of the time, Pallas kernels for 0%

commit v1 on v0

v1 whole, which is shorter than its diff:
```python
import functools

import jax
import jax.numpy as jnp
from jax import lax
from jax.experimental import pallas as pl
from jax.experimental.pallas import tpu as pltpu
from jax.sharding import PartitionSpec as P

THERMAL = 0.3
SLOTS = 32
FIRST_SLOTS = 16
GROUP = 4
ENTRY_BITS = 5

VMEM = pl.BlockSpec(memory_space=pltpu.VMEM)
SMEM = pl.BlockSpec(memory_space=pltpu.SMEM)
ANY = pl.BlockSpec(memory_space=pl.ANY)


def stage_body(stage, first, reach, layout, n_pieces, n_extra, *refs):
    plan_in, dipole = refs[:2]
    pieces = refs[2 : 2 + n_pieces]
    refs = refs[2 + n_pieces + n_extra :]
    if not first:
        refs = refs[2:]
    moments, entries, _, plan, low, plan_sem, entry_sems, piece_sems = refs
    n_slots, comps, block, _ = entries.shape
    total, low_bits = layout

    plan_copy = pltpu.make_async_copy(plan_in, plan, plan_sem)
    plan_copy.start()
    offset = 0
    piece_copies = []
    for i, piece in enumerate(pieces):
        count = piece.shape[0]
        piece_copies.append(
            pltpu.make_async_copy(piece, low.at[pl.ds(offset, count)], piece_sems.at[i])
        )
        offset += count
    for copy in piece_copies:
        copy.start()
    if first:
        moments[...] = jnp.zeros_like(moments)
    blank = low.shape[0] - 1
    low[blank] = jnp.zeros(low.shape[1:], low.dtype)
    plan_copy.wait()

    begin = plan[total + stage]
    end = plan[total + stage + 1]
    ahead = jnp.minimum(begin + reach[stage], total)
    if first:
        ready = begin
    else:
        ready = jnp.maximum(jnp.minimum(plan[total + stage - 1] + reach[stage - 1], total), begin)

    def place(pos):
        return pos & (n_slots - 1) if n_slots & (n_slots - 1) == 0 else lax.rem(pos, n_slots)

    def row(code):
        return code >> (low_bits + ENTRY_BITS)

    def load(pos):
        code = plan[pos]
        slot = place(pos)
        entry = (code >> low_bits) & ((1 << ENTRY_BITS) - 1)
        return pltpu.make_async_copy(dipole.at[row(code), entry], entries.at[slot], entry_sems.at[slot])

    @pl.loop(ready, ahead)
    def _(pos):
        load(pos).start()

    for copy in piece_copies:
        copy.wait()

    def work(start):
        positions = [start + i for i in range(GROUP)]

        @pl.when(start + GROUP > ready)
        def _():
            for pos in positions:
                @pl.when((pos >= ready) & (pos < end))
                def _(pos=pos):
                    load(pos).wait()

        kept = [jnp.minimum(pos, end - 1) for pos in positions]
        codes = [plan[pos] for pos in kept]
        rows = [row(code) for code in codes]
        picks = [
            jnp.where(pos < end, code & ((1 << low_bits) - 1), blank) for pos, code in zip(positions, codes)
        ]
        blocks = [low[pick] for pick in picks]
        for a in range(comps):
            products = [
                jnp.dot(entries[place(pos), a], lower, preferred_element_type=jnp.float32)
                for pos, lower in zip(kept, blocks)
            ]
            for r, product in zip(rows, products):
                moments[r, pl.ds(a * block, block)] += product

        @pl.when(start + n_slots < end)
        def _():
            for pos in positions:
                @pl.when(pos + n_slots < end)
                def _(pos=pos):
                    load(pos + n_slots).start()

    if pieces:
        @pl.loop(0, (end - begin + GROUP - 1) // GROUP)
        def _(g):
            work(begin + g * GROUP)

    @pl.loop(jnp.maximum(ready, end), ahead)
    def _(pos):
        load(pos).wait()


def split_halves(sums, bits, level, keep, send):
    comps, count, share, lower_count = sums.shape
    halves = sums.reshape(comps, count // 2, 2, share, lower_count)
    side = jnp.broadcast_to(bits[level][None, None, :1], (comps, count // 2, share, lower_count)) > 0
    keep[...] = jnp.where(side, halves[:, :, 1], halves[:, :, 0])
    send[...] = jnp.where(side, halves[:, :, 0], halves[:, :, 1])


def project(upper_t, moments, comps, lay):
    rows, height, _ = moments.shape
    block = height // comps
    span = min(4, rows)
    sums = []
    for a in range(comps):
        acc = None
        for r in range(0, rows, span):
            parts = [moments[r + i, pl.ds(a * block, block)] for i in range(span)]
            wide = jnp.concatenate(parts, axis=0)
            high = wide.astype(jnp.bfloat16)
            rest = (wide - high.astype(jnp.float32)).astype(jnp.bfloat16)
            both = jnp.concatenate([high, rest], axis=1)
            term = jnp.dot(
                upper_t[:, pl.ds(r * block, span * block)], both, preferred_element_type=jnp.float32
            )
            acc = term if acc is None else acc + term
        half = acc.shape[1] // 2
        sums.append((acc[:, :half] + acc[:, half:]).reshape(lay + (half,)))
    return jnp.stack(sums)


def small_call(body, out_shape, *operands):
    return pl.pallas_call(
        body,
        out_shape=out_shape,
        in_specs=[VMEM] * len(operands),
        out_specs=jax.tree.map(lambda _: VMEM, out_shape),
        compiler_params=pltpu.CompilerParams(vmem_limit_bytes=8 * 2**20),
    )(*operands)


def own_outputs(upper_t, moments, comps, bits, factor, group):
    upper_count = upper_t.shape[0]
    lower_count = moments.shape[2]
    share = upper_count // group
    levels = bits.shape[0]

    def shapes(count):
        return [jax.ShapeDtypeStruct((comps, count, share, lower_count), jnp.float32)] * 2

    def first(upper_t, moments, bits, keep, send):
        split_halves(project(upper_t, moments, comps, (group, share)), bits, 0, keep, send)

    def middle(level, held, other, bits, keep, send):
        split_halves(held[...] + other[...], bits, level, keep, send)

    def final(held, other, factor, strength, intensity):
        own = (held[...] + other[...])[:, 0]
        strength[...] = jnp.sum(own * own, axis=0)
        intensity[...] = factor[...] * strength[...]

    keep, send = small_call(first, shapes(group // 2), upper_t, moments, bits)
    for level in range(levels):
        bit = 1 << level
        other = lax.ppermute(send, "blk", [(d, d ^ bit) for d in range(group)])
        if level + 1 < levels:
            count = group >> (level + 2)
            keep, send = small_call(
                functools.partial(middle, level + 1), shapes(count), keep, other, bits
            )
    out = [jax.ShapeDtypeStruct((share, lower_count), jnp.float32)] * 2
    return small_call(final, out, keep, other, factor)


def run_stage(stage, reach, plan, layout, dipole, pieces, lower_count, state, needed=()):
    rows, _, comps, block, _ = dipole.shape
    first = state is None
    low_blocks = sum(p.shape[0] for p in pieces) + 1
    n_slots = min(SLOTS, layout[0])
    operands = [plan, dipole, *pieces, *needed]
    in_specs = [ANY] * len(operands)
    aliases = {}
    if not first:
        aliases = {len(operands): 0, len(operands) + 1: 1}
        operands += list(state)
        in_specs += [VMEM, VMEM]
    entries = layout[0] / 16
    result = pl.pallas_call(
        functools.partial(stage_body, stage, first, reach, layout, len(pieces), len(needed)),
        out_shape=[
            pltpu.VMEM((rows, comps * block, lower_count), jnp.float32),
            pltpu.VMEM((n_slots, comps, block, block), jnp.bfloat16),
            jax.ShapeDtypeStruct((8, 128), jnp.float32),
        ],
        in_specs=in_specs,
        out_specs=[VMEM, VMEM, ANY],
        input_output_aliases=aliases,
        scratch_shapes=[
            pltpu.SMEM(plan.shape, jnp.int32),
            pltpu.VMEM((low_blocks, block, lower_count), jnp.bfloat16),
            pltpu.SemaphoreType.DMA,
            pltpu.SemaphoreType.DMA((n_slots,)),
            pltpu.SemaphoreType.DMA((max(len(pieces), 1),)),
        ],
        cost_estimate=pl.CostEstimate(
            flops=int(entries * comps * block * block * lower_count * 2),
            bytes_accessed=int(entries * comps * block * block * 2),
            transcendentals=0,
        ),
        compiler_params=pltpu.CompilerParams(vmem_limit_bytes=(8 if low_blocks < 64 else 30) * 2**20),
    )(*operands)
    return result[:2], result[2]


def after(done, array):
    return pl.pallas_call(
        lambda *refs: None,
        out_shape=jax.ShapeDtypeStruct(array.shape, array.dtype),
        in_specs=[ANY, ANY],
        out_specs=ANY,
        input_output_aliases={0: 0},
        compiler_params=pltpu.CompilerParams(has_side_effects=True, vmem_limit_bytes=2**20),
    )(array, done)


def sorted_entries(stage, slot, n_stages, low_bits):
    rows, count = stage.shape
    total = rows * count
    row = lax.broadcasted_iota(jnp.int32, stage.shape, 0)
    entry = lax.broadcasted_iota(jnp.int32, stage.shape, 1)
    code = ((((row << ENTRY_BITS) + entry) << low_bits) + slot).reshape(total)
    key = (stage * total + row * count + entry).reshape(total)
    rank = jnp.sum((key[None, :] < key[:, None]).astype(jnp.int32), axis=1)
    length = -(-(total + n_stages + 1) // 128) * 128
    place = jnp.arange(length, dtype=jnp.int32)
    codes = jnp.sum(jnp.where(rank[:, None] == place[None, :], code[:, None], 0), axis=0)
    bounds = jnp.sum((stage.reshape(total, 1) < place[None, :] - total).astype(jnp.int32), axis=0)
    return jnp.where(place < total, codes, bounds)


def ring_moments(dipole, block_cols, lower_blocks, group, needed):
    rows = dipole.shape[0]
    lower_count = lower_blocks.shape[2]
    me = lax.axis_index("blk")
    chips = group // 2
    order = [c for c in range(0, chips, 2)] + [c for c in range(chips - 1, 0, -2)]
    steps = [(order[i], order[(i + 1) % chips]) for i in range(chips)]
    ways = [
        [(2 * a, 2 * b) for a, b in steps] + [(2 * b + 1, 2 * a + 1) for a, b in steps],
        [(2 * b, 2 * a) for a, b in steps] + [(2 * a + 1, 2 * b + 1) for a, b in steps],
    ]
    sibling = [(d, d ^ 1) for d in range(group)]
    half = rows // 2

    def position(device):
        chip = device // 2
        return jnp.where(chip % 2 == 0, chip // 2, chips - 1 - chip // 2)

    owner = block_cols // rows
    local = block_cols % rows
    part = local // half
    forward = (part + owner) % 2 == 0
    mine, theirs = position(me), position(owner)
    hops = jnp.where(forward, mine - theirs, theirs - mine) % chips
    other_core = (owner + me) % 2
    stage = jnp.where(hops == 0, 1, 2 * hops + part)
    slot = jnp.where(hops == 0, other_core * rows + local, other_core * half + local % half)
    n_stages = 2 * chips
    layout = (block_cols.size, (2 * rows - 1).bit_length())
    plan = sorted_entries(stage, slot, n_stages, layout[1])
    reach = [FIRST_SLOTS] + [SLOTS] * (n_stages - 1)

    def hop(array, p):
        return lax.ppermute(array, "blk", ways[p])

    def cross(array):
        return [array, lax.ppermute(array, "blk", sibling)]

    def compute(number, arrived, state, needed=()):
        return run_stage(number, reach, plan, layout, dipole, arrived, lower_count, state, needed)

    flying = [hop(lower_blocks[p * half : (p + 1) * half], p) for p in range(2)]
    waiting = (1, cross(lower_blocks))
    state, done = compute(0, [], None, needed)
    for h in range(1, chips):
        for p in range(2):
            here = after(done, flying[p])
            if h < chips - 1:
                flying[p] = hop(here, p)
            here = cross(here)
            state, done = compute(*waiting, state)
            waiting = (2 * h + p, here)
    state, done = compute(*waiting, state)
    return state[0]


def gathered_moments(dipole, block_cols, lower_blocks):
    gathered = lax.all_gather(lower_blocks, "blk", axis=0, tiled=True)
    layout = (block_cols.size, (gathered.shape[0] - 1).bit_length())
    plan = sorted_entries(jnp.zeros_like(block_cols), block_cols, 1, layout[1])
    state, _ = run_stage(0, [SLOTS], plan, layout, dipole, [gathered], lower_blocks.shape[2], None)
    return state[0]


def own_rows(proj, group):
    me = lax.axis_index("blk")
    comps, upper_count, lower_count = proj.shape
    share = upper_count // group
    held = proj.reshape(comps, group, share, lower_count)
    bit = 1
    while bit < group:
        halves = held.reshape(comps, held.shape[1] // 2, 2, share, lower_count)
        side = (me // bit) % 2
        keep = lax.dynamic_index_in_dim(halves, side, 2, keepdims=False)
        send = lax.dynamic_index_in_dim(halves, 1 - side, 2, keepdims=False)
        held = keep + lax.ppermute(send, "blk", [(d, d ^ bit) for d in range(group)])
        bit *= 2
    return held[:, 0]


def per_device(dipole, block_cols, upper_vecs, lower_vecs, upper_energy, lower_energy):
    rows, _, _, block, _ = dipole.shape
    group = lax.axis_size("blk")
    me = lax.axis_index("blk")
    lower_blocks = lower_vecs.reshape(rows, block, lower_vecs.shape[1])
    upper_t = upper_vecs.T
    share = upper_vecs.shape[1] // group
    energy = lax.dynamic_slice_in_dim(upper_energy, me * share, share, 0)
    wavenumber = energy[:, None] - lower_energy[None, :]
    factor = wavenumber**3 * jnp.exp(-lower_energy / THERMAL)[None, :]
    comps = dipole.shape[2]
    if rows % 2 == 0 and share % 8 == 0 and group >= 8 and group & (group - 1) == 0:
        levels = jnp.arange(group.bit_length() - 1, dtype=jnp.int32)
        bits = jnp.broadcast_to(((me >> levels) & 1)[:, None, None], (levels.shape[0], 8, 128))
        needed = [upper_t, factor, bits]
        moments = ring_moments(dipole, block_cols, lower_blocks, group, needed)
        return own_outputs(upper_t, moments, comps, bits, factor, group)
    moments = gathered_moments(dipole, block_cols, lower_blocks)

    def body(upper_t, moments, proj):
        proj[...] = project(upper_t, moments, comps, (upper_t.shape[0],))

    shape = jax.ShapeDtypeStruct((comps, upper_t.shape[0], lower_blocks.shape[2]), jnp.float32)
    own = own_rows(small_call(body, shape, upper_t, moments), group)
    strength = jnp.sum(own * own, axis=0)
    return strength, factor * strength


def solution(mesh):
    placed = (
        P("blk", None, None, None, None),
        P("blk", None),
        P(("jpair", "blk"), None),
        P(("jpair", "blk"), None),
        P("jpair"),
        P("jpair"),
    )
    return jax.shard_map(
        per_device,
        mesh=mesh,
        in_specs=placed,
        out_specs=(P(("jpair", "blk"), None), P(("jpair", "blk"), None)),
        check_vma=False,
    )
```

time: 284 us -> 119 us (0.42)
  waiting for transfers between devices: 160 us -> 13.7 us
  matrix products: 91.9 us -> 0 us
  Pallas kernels: 0 us -> 59.2 us
  starting transfers between devices: 0.08 us -> 36.9 us
  between operations: 14.1 us -> 1.14 us
  local copies, waits for them, and re-layouts: 16.3 us -> 5.6 us
    dot_general x2 -> x0, matrix products: 91.9 us -> none  [the longest x1 59 us: per_device(): jnp.einsum('rkast,rsu->rkatu', dipole, upper_blocks, preferred_element_ty...]
    psum x1 -> x0, waiting for transfers between devices: 88.6 us -> none  [per_device(): summed = lax.psum(proj, 'blk')]
    all_gather x1 -> x0, waiting for transfers between devices: 70.4 us -> none  [per_device(): gathered = lax.all_gather(lower_vecs, 'blk', axis=0, tiled=True)]
    pallas_call x0 -> x35, Pallas kernels: none -> 59.2 us  [the longest x16 56.7 us: run_stage(): pl.pallas_call(functools.partial(stage_body, stage, first, reach, layout,...]
    ppermute x0 -> x33, starting transfers between devices: none -> 36.9 us  [the longest x14 27.3 us: hop(): return lax.ppermute(array, 'blk', ways[p])]
    gather x1 -> x0, local copies, waits for them, and re-layouts: 13.9 us -> none  [per_device(): lows = jnp.take(all_blocks, columns, axis=0)]
    ppermute x0 -> x33, waiting for transfers between devices: none -> 13.7 us  [the longest x4 9.46 us: own_outputs(): other = lax.ppermute(send, 'blk', [(d, d ^ bit) for d in range(group)])]
    unnamed x6 -> x15, local copies, waits for them, and re-layouts: 0.02 us -> 2.95 us
  transfers between devices with their start and end apart: 2 -> 33, of which waited for: 2 -> 9; matrix products, arithmetic and copies ran while one was open for 22% -> 6% of each run, Pallas kernels for 0% -> 45%
where the time goes in v1:
time: 119 us
  Pallas kernels  59.2 us (50%)
  starting transfers between devices  36.9 us (31%)
  waiting for transfers between devices  13.7 us (12%)
  local copies, waits for them, and re-layouts  5.6 us (5%)
  other arithmetic  1.99 us (2%)
    pallas_call x16, Pallas kernels, run_stage(): pl.pallas_call(functools.partial(stage_body, stage, first, reach, layout,...  56.7 us
    ppermute x14, starting transfers between devices, hop(): return lax.ppermute(array, 'blk', ways[p])  27.3 us
    ppermute x4, waiting for transfers between devices, own_outputs(): other = lax.ppermute(send, 'blk', [(d, d ^ bit) for d in range(group)])  9.46 us
    ppermute x4, starting transfers between devices, own_outputs(): other = lax.ppermute(send, 'blk', [(d, d ^ bit) for d in range(group)])  6.65 us
    ppermute x14, waiting for transfers between devices, hop(): return lax.ppermute(array, 'blk', ways[p])  4.21 us
    unnamed x15, local copies, waits for them, and re-layouts  2.95 us
    ppermute x15, starting transfers between devices, cross(): return [array, lax.ppermute(array, 'blk', sibling)]  2.95 us
    pallas_call x5, Pallas kernels, small_call(): pl.pallas_call(body, out_shape=out_shape, in_specs=[VMEM] * len(operands)...  2.45 us
  transfers between devices with their start and end apart: 33, of which 9 were waited for; matrix products, arithmetic and copies ran while one was open for 6% of the time, Pallas kernels for 45%

profile of v1, /device:TPU:0, one launch (start us, length us, event | category | flops | bytes accessed | tf_op | source)
XLA Modules:
  0.0 118.6 jit_solution(16492819524282896810)
XLA Ops:
  3.4 2.6 %collective-permute-start.4 = (bf16[8,256,128]{2,1,0:T(8,128)(2,1)}, bf16[8,256,128]{2,1,0:T(8,128)(2,1)S(1)}, u32[]{:S(2)}, u32[]{:S(2)}) collective-permute-start(bf16[8,256,128]{2,1,0:T(8,128)(2,1)} %bitcast.3), channel_id=1, source_target_pairs={{0,4},{4,8},{8,12},{12,14},{14,10},{10,6},{6,2},{2,0},{5,1},{9,5},... | collective-permute-start | bytes 1572872 | tf_op jit(solution)/shard_map/ppermute | solution.py:290
  8.2 2.9 %copy.53 = bf16[4096,256]{0,1:T(8,128)(2,1)S(1)} copy(bf16[4096,256]{1,0:T(8,128)(2,1)} %param.8) | data formatting | bytes 4194304 | tf_op args[2]
  11.4 3.7 %shard_map.77 = (f32[16,768,128]{2,1,0:T(8,128)S(1)}, bf16[32,3,256,256]{3,2,1,0:T(8,128)(2,1)S(1)}, f32[8,128]{1,0:T(8,128)S(1)}) custom-call(s32[256]{0:T(256)S(1)} %compare_select_fusion.refs_0_, bf16[16,12,3,256,256]{4,3,2,1,0:T(8,128)(2,1)} %refs_1_.31, bf16[256,4096]{1,0:T(8,128)(2,1)S(1)} %bitcast.4, f32[16,128]{1,0:T(8,128)S(1)} %fusion.9.refs_3_.factor, ...), custom_call_target="tpu_custom_call" | custom-call | flops 603979776 | bytes 4718592 | tf_op jit(solution)/shard_map/pallas_call | solution.py:204
  15.1 3.0 %collective-permute-done.4.refs_0_ = bf16[8,256,128]{2,1,0:T(8,128)(2,1)S(1)} collective-permute-done((bf16[8,256,128]{2,1,0:T(8,128)(2,1)}, bf16[8,256,128]{2,1,0:T(8,128)(2,1)S(1)}, u32[]{:S(2)}, u32[]{:S(2)}) %collective-permute-start.4) | collective-permute-done | bytes 524320 | tf_op jit(solution)/shard_map/ppermute | solution.py:290
  20.5 5.7 %shard_map.78 = (f32[16,768,128]{2,1,0:T(8,128)S(1)}, bf16[32,3,256,256]{3,2,1,0:T(8,128)(2,1)S(1)}, f32[8,128]{1,0:T(8,128)S(1)}) custom-call(s32[256]{0:T(256)S(1)} %compare_select_fusion.refs_0_, bf16[16,12,3,256,256]{4,3,2,1,0:T(8,128)(2,1)} %refs_1_.31, bf16[16,256,128]{2,1,0:T(8,128)(2,1)S(1)} %bitcast.7, ...), custom_call_target="tpu_custom_call", output_to_operand_aliasing={{0}: (4, {}), {1}: (5, {})} | custom-call | flops 603979776 | bytes 4718592 | tf_op jit(solution)/shard_map/pallas_call | solution.py:204
  27.8 5.0 %shard_map.81 = (f32[16,768,128]{2,1,0:T(8,128)S(1)}, bf16[32,3,256,256]{3,2,1,0:T(8,128)(2,1)S(1)}, f32[8,128]{1,0:T(8,128)S(1)}) custom-call(s32[256]{0:T(256)S(1)} %compare_select_fusion.refs_0_, bf16[16,12,3,256,256]{4,3,2,1,0:T(8,128)(2,1)} %refs_1_.31, ...), custom_call_target="tpu_custom_call", output_to_operand_aliasing={{0}: (4, {}), {1}: (5, {})} | custom-call | flops 603979776 | bytes 4718592 | tf_op jit(solution)/shard_map/pallas_call | solution.py:204
  35.1 3.4 %shard_map.82 = (f32[16,768,128]{2,1,0:T(8,128)S(1)}, bf16[32,3,256,256]{3,2,1,0:T(8,128)(2,1)S(1)}, f32[8,128]{1,0:T(8,128)S(1)}) custom-call(s32[256]{0:T(256)S(1)} %compare_select_fusion.refs_0_, bf16[16,12,3,256,256]{4,3,2,1,0:T(8,128)(2,1)} %refs_1_.31, ...), custom_call_target="tpu_custom_call", output_to_operand_aliasing={{0}: (4, {}), {1}: (5, {})} | custom-call | flops 603979776 | bytes 4718592 | tf_op jit(solution)/shard_map/pallas_call | solution.py:204
  39.9 3.6 %shard_map.85 = (f32[16,768,128]{2,1,0:T(8,128)S(1)}, bf16[32,3,256,256]{3,2,1,0:T(8,128)(2,1)S(1)}, f32[8,128]{1,0:T(8,128)S(1)}) custom-call(s32[256]{0:T(256)S(1)} %compare_select_fusion.refs_0_, bf16[16,12,3,256,256]{4,3,2,1,0:T(8,128)(2,1)} %refs_1_.31, ...), custom_call_target="tpu_custom_call", output_to_operand_aliasing={{0}: (4, {}), {1}: (5, {})} | custom-call | flops 603979776 | bytes 4718592 | tf_op jit(solution)/shard_map/pallas_call | solution.py:204
  46.0 2.8 %shard_map.86 = (f32[16,768,128]{2,1,0:T(8,128)S(1)}, bf16[32,3,256,256]{3,2,1,0:T(8,128)(2,1)S(1)}, f32[8,128]{1,0:T(8,128)S(1)}) custom-call(s32[256]{0:T(256)S(1)} %compare_select_fusion.refs_0_, bf16[16,12,3,256,256]{4,3,2,1,0:T(8,128)(2,1)} %refs_1_.31, ...), custom_call_target="tpu_custom_call", output_to_operand_aliasing={{0}: (4, {}), {1}: (5, {})} | custom-call | flops 603979776 | bytes 4718592 | tf_op jit(solution)/shard_map/pallas_call | solution.py:204
  51.7 3.4 %shard_map.89 = (f32[16,768,128]{2,1,0:T(8,128)S(1)}, bf16[32,3,256,256]{3,2,1,0:T(8,128)(2,1)S(1)}, f32[8,128]{1,0:T(8,128)S(1)}) custom-call(s32[256]{0:T(256)S(1)} %compare_select_fusion.refs_0_, bf16[16,12,3,256,256]{4,3,2,1,0:T(8,128)(2,1)} %refs_1_.31, ...), custom_call_target="tpu_custom_call", output_to_operand_aliasing={{0}: (4, {}), {1}: (5, {})} | custom-call | flops 603979776 | bytes 4718592 | tf_op jit(solution)/shard_map/pallas_call | solution.py:204
  57.5 3.3 %shard_map.90 = (f32[16,768,128]{2,1,0:T(8,128)S(1)}, bf16[32,3,256,256]{3,2,1,0:T(8,128)(2,1)S(1)}, f32[8,128]{1,0:T(8,128)S(1)}) custom-call(s32[256]{0:T(256)S(1)} %compare_select_fusion.refs_0_, bf16[16,12,3,256,256]{4,3,2,1,0:T(8,128)(2,1)} %refs_1_.31, ...), custom_call_target="tpu_custom_call", output_to_operand_aliasing={{0}: (4, {}), {1}: (5, {})} | custom-call | flops 603979776 | bytes 4718592 | tf_op jit(solution)/shard_map/pallas_call | solution.py:204
  60.9 2.7 %collective-permute-start.14 = (bf16[8,256,128]{2,1,0:T(8,128)(2,1)S(1)}, bf16[8,256,128]{2,1,0:T(8,128)(2,1)S(1)}, u32[]{:S(2)}, u32[]{:S(2)}) collective-permute-start(bf16[8,256,128]{2,1,0:T(8,128)(2,1)S(1)} %shard_map.91.refs_2_), channel_id=1, source_target_pairs={{4,0},{8,4},{12,8},{14,12},{10,14},{6,10},{2,6},{0,2},{1,5},{5,9},... | collective-permute-start | bytes 1572872 | tf_op jit(solution)/shard_map/ppermute | solution.py:290
  63.6 3.4 %shard_map.93 = (f32[16,768,128]{2,1,0:T(8,128)S(1)}, bf16[32,3,256,256]{3,2,1,0:T(8,128)(2,1)S(1)}, f32[8,128]{1,0:T(8,128)S(1)}) custom-call(s32[256]{0:T(256)S(1)} %compare_select_fusion.refs_0_, bf16[16,12,3,256,256]{4,3,2,1,0:T(8,128)(2,1)} %refs_1_.31, ...), custom_call_target="tpu_custom_call", output_to_operand_aliasing={{0}: (4, {}), {1}: (5, {})} | custom-call | flops 603979776 | bytes 4718592 | tf_op jit(solution)/shard_map/pallas_call | solution.py:204
  68.8 3.4 %shard_map.94 = (f32[16,768,128]{2,1,0:T(8,128)S(1)}, bf16[32,3,256,256]{3,2,1,0:T(8,128)(2,1)S(1)}, f32[8,128]{1,0:T(8,128)S(1)}) custom-call(s32[256]{0:T(256)S(1)} %compare_select_fusion.refs_0_, bf16[16,12,3,256,256]{4,3,2,1,0:T(8,128)(2,1)} %refs_1_.31, ...), custom_call_target="tpu_custom_call", output_to_operand_aliasing={{0}: (4, {}), {1}: (5, {})} | custom-call | flops 603979776 | bytes 4718592 | tf_op jit(solution)/shard_map/pallas_call | solution.py:204
  72.5 2.7 %collective-permute-start.18 = (bf16[8,256,128]{2,1,0:T(8,128)(2,1)S(1)}, bf16[8,256,128]{2,1,0:T(8,128)(2,1)S(1)}, u32[]{:S(2)}, u32[]{:S(2)}) collective-permute-start(bf16[8,256,128]{2,1,0:T(8,128)(2,1)S(1)} %shard_map.95.refs_2_), channel_id=1, source_target_pairs={{4,0},{8,4},{12,8},{14,12},{10,14},{6,10},{2,6},{0,2},{1,5},{5,9},... | collective-permute-start | bytes 1572872 | tf_op jit(solution)/shard_map/ppermute | solution.py:290
  75.2 3.0 %shard_map.97 = (f32[16,768,128]{2,1,0:T(8,128)S(1)}, bf16[32,3,256,256]{3,2,1,0:T(8,128)(2,1)S(1)}, f32[8,128]{1,0:T(8,128)S(1)}) custom-call(s32[256]{0:T(256)S(1)} %compare_select_fusion.refs_0_, bf16[16,12,3,256,256]{4,3,2,1,0:T(8,128)(2,1)} %refs_1_.31, ...), custom_call_target="tpu_custom_call", output_to_operand_aliasing={{0}: (4, {}), {1}: (5, {})} | custom-call | flops 603979776 | bytes 4718592 | tf_op jit(solution)/shard_map/pallas_call | solution.py:204
  80.2 3.1 %shard_map.98 = (f32[16,768,128]{2,1,0:T(8,128)S(1)}, bf16[32,3,256,256]{3,2,1,0:T(8,128)(2,1)S(1)}, f32[8,128]{1,0:T(8,128)S(1)}) custom-call(s32[256]{0:T(256)S(1)} %compare_select_fusion.refs_0_, bf16[16,12,3,256,256]{4,3,2,1,0:T(8,128)(2,1)} %refs_1_.31, ...), custom_call_target="tpu_custom_call", output_to_operand_aliasing={{0}: (4, {}), {1}: (5, {})} | custom-call | flops 603979776 | bytes 4718592 | tf_op jit(solution)/shard_map/pallas_call | solution.py:204
  84.0 2.5 %collective-permute-start.22 = (bf16[8,256,128]{2,1,0:T(8,128)(2,1)S(1)}, bf16[8,256,128]{2,1,0:T(8,128)(2,1)S(1)}, u32[]{:S(2)}, u32[]{:S(2)}) collective-permute-start(bf16[8,256,128]{2,1,0:T(8,128)(2,1)S(1)} %shard_map.99.refs_2_), channel_id=1, source_target_pairs={{4,0},{8,4},{12,8},{14,12},{10,14},{6,10},{2,6},{0,2},{1,5},{5,9},... | collective-permute-start | bytes 1572872 | tf_op jit(solution)/shard_map/ppermute | solution.py:290
  86.5 3.4 %shard_map.101 = (f32[16,768,128]{2,1,0:T(8,128)S(1)}, bf16[32,3,256,256]{3,2,1,0:T(8,128)(2,1)S(1)}, f32[8,128]{1,0:T(8,128)S(1)}) custom-call(s32[256]{0:T(256)S(1)} %compare_select_fusion.refs_0_, bf16[16,12,3,256,256]{4,3,2,1,0:T(8,128)(2,1)} %refs_1_.31, ...), custom_call_target="tpu_custom_call", output_to_operand_aliasing={{0}: (4, {}), {1}: (5, {})} | custom-call | flops 603979776 | bytes 4718592 | tf_op jit(solution)/shard_map/pallas_call | solution.py:204
  90.1 3.5 %shard_map.102 = (f32[16,768,128]{2,1,0:T(8,128)S(1)}, bf16[32,3,256,256]{3,2,1,0:T(8,128)(2,1)S(1)}, f32[8,128]{1,0:T(8,128)S(1)}) custom-call(s32[256]{0:T(256)S(1)} %compare_select_fusion.refs_0_, bf16[16,12,3,256,256]{4,3,2,1,0:T(8,128)(2,1)} %refs_1_.31, ...), custom_call_target="tpu_custom_call", output_to_operand_aliasing={{0}: (4, {}), {1}: (5, {})} | custom-call | flops 603979776 | bytes 4718592 | tf_op jit(solution)/shard_map/pallas_call | solution.py:204
  93.8 2.8 %shard_map.105 = (f32[16,768,128]{2,1,0:T(8,128)S(1)}, bf16[32,3,256,256]{3,2,1,0:T(8,128)(2,1)S(1)}, f32[8,128]{1,0:T(8,128)}) custom-call(s32[256]{0:T(256)S(1)} %compare_select_fusion.refs_0_, bf16[16,12,3,256,256]{4,3,2,1,0:T(8,128)(2,1)} %refs_1_.31, bf16[8,256,128]{2,1,0:T(8,128)(2,1)S(1)} %shard_map.104.refs_2_, ...), custom_call_target="tpu_custom_call", output_to_operand_aliasing={{0}: (4, {}), {1}: (5, {})} | custom-call | flops 603979776 | bytes 4718592 | tf_op jit(solution)/shard_map/pallas_call | solution.py:204
  96.7 3.3 %shard_map.106 = (f32[16,768,128]{2,1,0:T(8,128)S(1)}, bf16[32,3,256,256]{3,2,1,0:T(8,128)(2,1)S(1)}, f32[8,128]{1,0:T(8,128)}) custom-call(s32[256]{0:T(256)S(1)} %compare_select_fusion.refs_0_, bf16[16,12,3,256,256]{4,3,2,1,0:T(8,128)(2,1)} %refs_1_.31, bf16[8,256,128]{2,1,0:T(8,128)(2,1)S(1)} %shard_map.103.refs_2_, ...), custom_call_target="tpu_custom_call", output_to_operand_aliasing={{0}: (4, {}), {1}: (5, {})} | custom-call | flops 603979776 | bytes 4718592 | tf_op jit(solution)/shard_map/pallas_call | solution.py:204
  105.3 3.7 %collective-permute-done.30.other = f32[3,4,16,128]{3,2,1,0:T(8,128)S(1)} collective-permute-done((f32[3,4,16,128]{3,2,1,0:T(8,128)S(1)}, f32[3,4,16,128]{3,2,1,0:T(8,128)S(1)}, u32[]{:S(2)}, u32[]{:S(2)}) %collective-permute-start.30) | collective-permute-done | bytes 98336 | tf_op jit(solution)/shard_map/ppermute | solution.py:181
  115.5 2.4 %collective-permute-done.32.other = f32[3,1,16,128]{3,2,1,0:T(8,128)S(1)} collective-permute-done((f32[3,1,16,128]{3,2,1,0:T(8,128)S(1)}, f32[3,1,16,128]{3,2,1,0:T(8,128)S(1)}, u32[]{:S(2)}, u32[]{:S(2)}) %collective-permute-start.32) | collective-permute-done | bytes 24608 | tf_op jit(solution)/shard_map/ppermute | solution.py:181
  (109 shorter events, 38.2 us)
Async XLA Ops:
  0.6 19.9 %collective-permute-start.1 = (bf16[16,256,128]{2,1,0:T(8,128)(2,1)}, bf16[16,256,128]{2,1,0:T(8,128)(2,1)}, u32[]{:S(2)}, u32[]{:S(2)}) collective-permute-start(bf16[16,256,128]{2,1,0:T(8,128)(2,1)} %bitcast.6), channel_id=1, source_target_pairs={{0,1},{1,0},{2,3},{3,2},{4,5},{5,4},{6,7},{7,6},{8,9},{9,8},{10,11... | collective-permute-start | bytes 3145736 | tf_op jit(solution)/shard_map/ppermute | solution.py:293
  3.4 14.7 %collective-permute-start.4 = (bf16[8,256,128]{2,1,0:T(8,128)(2,1)}, bf16[8,256,128]{2,1,0:T(8,128)(2,1)S(1)}, u32[]{:S(2)}, u32[]{:S(2)}) collective-permute-start(bf16[8,256,128]{2,1,0:T(8,128)(2,1)} %bitcast.3), channel_id=1, source_target_pairs={{0,4},{4,8},{8,12},{12,14},{14,10},{10,6},{6,2},{2,0},{5,1},{9,5},... | collective-permute-start | bytes 1572872 | tf_op jit(solution)/shard_map/ppermute | solution.py:290
  6.0 20.3 %collective-permute-start = (bf16[8,256,128]{2,1,0:T(8,128)(2,1)}, bf16[8,256,128]{2,1,0:T(8,128)(2,1)S(1)}, u32[]{:S(2)}, u32[]{:S(2)}) collective-permute-start(bf16[8,256,128]{2,1,0:T(8,128)(2,1)} %bitcast.1), channel_id=1, source_target_pairs={{4,0},{8,4},{12,8},{14,12},{10,14},{6,10},{2,6},{0,2},{1,5},{5,9},... | collective-permute-start | bytes 1572872 | tf_op jit(solution)/shard_map/ppermute | solution.py:290
  18.2 9.7 %collective-permute-start.5 = (bf16[8,256,128]{2,1,0:T(8,128)(2,1)S(1)}, bf16[8,256,128]{2,1,0:T(8,128)(2,1)S(1)}, u32[]{:S(2)}, u32[]{:S(2)}) collective-permute-start(bf16[8,256,128]{2,1,0:T(8,128)(2,1)S(1)} %shard_map.80.refs_2_), channel_id=1, source_target_pairs={{0,1},{1,0},{2,3},{3,2},{4,5},{5,4},{6,7},{7,6},{8,9},{9,8},{10,11... | collective-permute-start | bytes 1572872 | tf_op jit(solution)/shard_map/ppermute | solution.py:293
  18.2 14.7 %collective-permute-start.8 = (bf16[8,256,128]{2,1,0:T(8,128)(2,1)S(1)}, bf16[8,256,128]{2,1,0:T(8,128)(2,1)S(1)}, u32[]{:S(2)}, u32[]{:S(2)}) collective-permute-start(bf16[8,256,128]{2,1,0:T(8,128)(2,1)S(1)} %shard_map.80.refs_2_), channel_id=1, source_target_pairs={{0,4},{4,8},{8,12},{12,14},{14,10},{10,6},{6,2},{2,0},{5,1},{9,5},... | collective-permute-start | bytes 1572872 | tf_op jit(solution)/shard_map/ppermute | solution.py:290
  26.3 8.8 %collective-permute-start.3 = (bf16[8,256,128]{2,1,0:T(8,128)(2,1)S(1)}, bf16[8,256,128]{2,1,0:T(8,128)(2,1)S(1)}, u32[]{:S(2)}, u32[]{:S(2)}) collective-permute-start(bf16[8,256,128]{2,1,0:T(8,128)(2,1)S(1)} %shard_map.79.refs_2_), channel_id=1, source_target_pairs={{0,1},{1,0},{2,3},{3,2},{4,5},{5,4},{6,7},{7,6},{8,9},{9,8},{10,11... | collective-permute-start | bytes 1572872 | tf_op jit(solution)/shard_map/ppermute | solution.py:293
  26.4 12.0 %collective-permute-start.2 = (bf16[8,256,128]{2,1,0:T(8,128)(2,1)S(1)}, bf16[8,256,128]{2,1,0:T(8,128)(2,1)S(1)}, u32[]{:S(2)}, u32[]{:S(2)}) collective-permute-start(bf16[8,256,128]{2,1,0:T(8,128)(2,1)S(1)} %shard_map.79.refs_2_), channel_id=1, source_target_pairs={{4,0},{8,4},{12,8},{14,12},{10,14},{6,10},{2,6},{0,2},{1,5},{5,9},... | collective-permute-start | bytes 1572872 | tf_op jit(solution)/shard_map/ppermute | solution.py:290
  33.5 10.2 %collective-permute-start.12 = (bf16[8,256,128]{2,1,0:T(8,128)(2,1)S(1)}, bf16[8,256,128]{2,1,0:T(8,128)(2,1)S(1)}, u32[]{:S(2)}, u32[]{:S(2)}) collective-permute-start(bf16[8,256,128]{2,1,0:T(8,128)(2,1)S(1)} %shard_map.84.refs_2_), channel_id=1, source_target_pairs={{0,4},{4,8},{8,12},{12,14},{14,10},{10,6},{6,2},{2,0},{5,1},{9,5},... | collective-permute-start | bytes 1572872 | tf_op jit(solution)/shard_map/ppermute | solution.py:290
  38.5 10.2 %collective-permute-start.6 = (bf16[8,256,128]{2,1,0:T(8,128)(2,1)S(1)}, bf16[8,256,128]{2,1,0:T(8,128)(2,1)S(1)}, u32[]{:S(2)}, u32[]{:S(2)}) collective-permute-start(bf16[8,256,128]{2,1,0:T(8,128)(2,1)S(1)} %shard_map.83.refs_2_), channel_id=1, source_target_pairs={{4,0},{8,4},{12,8},{14,12},{10,14},{6,10},{2,6},{0,2},{1,5},{5,9},... | collective-permute-start | bytes 1572872 | tf_op jit(solution)/shard_map/ppermute | solution.py:290
  43.6 8.1 %collective-permute-start.13 = (bf16[8,256,128]{2,1,0:T(8,128)(2,1)S(1)}, bf16[8,256,128]{2,1,0:T(8,128)(2,1)S(1)}, u32[]{:S(2)}, u32[]{:S(2)}) collective-permute-start(bf16[8,256,128]{2,1,0:T(8,128)(2,1)S(1)} %shard_map.88.refs_2_), channel_id=1, source_target_pairs={{0,1},{1,0},{2,3},{3,2},{4,5},{5,4},{6,7},{7,6},{8,9},{9,8},{10,11... | collective-permute-start | bytes 1572872 | tf_op jit(solution)/shard_map/ppermute | solution.py:293
  43.7 11.5 %collective-permute-start.16 = (bf16[8,256,128]{2,1,0:T(8,128)(2,1)S(1)}, bf16[8,256,128]{2,1,0:T(8,128)(2,1)S(1)}, u32[]{:S(2)}, u32[]{:S(2)}) collective-permute-start(bf16[8,256,128]{2,1,0:T(8,128)(2,1)S(1)} %shard_map.88.refs_2_), channel_id=1, source_target_pairs={{0,4},{4,8},{8,12},{12,14},{14,10},{10,6},{6,2},{2,0},{5,1},{9,5},... | collective-permute-start | bytes 1572872 | tf_op jit(solution)/shard_map/ppermute | solution.py:290
  48.8 8.7 %collective-permute-start.11 = (bf16[8,256,128]{2,1,0:T(8,128)(2,1)S(1)}, bf16[8,256,128]{2,1,0:T(8,128)(2,1)S(1)}, u32[]{:S(2)}, u32[]{:S(2)}) collective-permute-start(bf16[8,256,128]{2,1,0:T(8,128)(2,1)S(1)} %shard_map.87.refs_2_), channel_id=1, source_target_pairs={{0,1},{1,0},{2,3},{3,2},{4,5},{5,4},{6,7},{7,6},{8,9},{9,8},{10,11... | collective-permute-start | bytes 1572872 | tf_op jit(solution)/shard_map/ppermute | solution.py:293
  49.4 11.4 %collective-permute-start.10 = (bf16[8,256,128]{2,1,0:T(8,128)(2,1)S(1)}, bf16[8,256,128]{2,1,0:T(8,128)(2,1)S(1)}, u32[]{:S(2)}, u32[]{:S(2)}) collective-permute-start(bf16[8,256,128]{2,1,0:T(8,128)(2,1)S(1)} %shard_map.87.refs_2_), channel_id=1, source_target_pairs={{4,0},{8,4},{12,8},{14,12},{10,14},{6,10},{2,6},{0,2},{1,5},{5,9},... | collective-permute-start | bytes 1572872 | tf_op jit(solution)/shard_map/ppermute | solution.py:290
  55.2 8.4 %collective-permute-start.17 = (bf16[8,256,128]{2,1,0:T(8,128)(2,1)S(1)}, bf16[8,256,128]{2,1,0:T(8,128)(2,1)S(1)}, u32[]{:S(2)}, u32[]{:S(2)}) collective-permute-start(bf16[8,256,128]{2,1,0:T(8,128)(2,1)S(1)} %shard_map.92.refs_2_), channel_id=1, source_target_pairs={{0,1},{1,0},{2,3},{3,2},{4,5},{5,4},{6,7},{7,6},{8,9},{9,8},{10,11... | collective-permute-start | bytes 1572872 | tf_op jit(solution)/shard_map/ppermute | solution.py:293
  55.2 11.8 %collective-permute-start.20 = (bf16[8,256,128]{2,1,0:T(8,128)(2,1)S(1)}, bf16[8,256,128]{2,1,0:T(8,128)(2,1)S(1)}, u32[]{:S(2)}, u32[]{:S(2)}) collective-permute-start(bf16[8,256,128]{2,1,0:T(8,128)(2,1)S(1)} %shard_map.92.refs_2_), channel_id=1, source_target_pairs={{0,4},{4,8},{8,12},{12,14},{14,10},{10,6},{6,2},{2,0},{5,1},{9,5},... | collective-permute-start | bytes 1572872 | tf_op jit(solution)/shard_map/ppermute | solution.py:290
  60.8 8.0 %collective-permute-start.15 = (bf16[8,256,128]{2,1,0:T(8,128)(2,1)S(1)}, bf16[8,256,128]{2,1,0:T(8,128)(2,1)S(1)}, u32[]{:S(2)}, u32[]{:S(2)}) collective-permute-start(bf16[8,256,128]{2,1,0:T(8,128)(2,1)S(1)} %shard_map.91.refs_2_), channel_id=1, source_target_pairs={{0,1},{1,0},{2,3},{3,2},{4,5},{5,4},{6,7},{7,6},{8,9},{9,8},{10,11... | collective-permute-start | bytes 1572872 | tf_op jit(solution)/shard_map/ppermute | solution.py:293
  60.9 11.6 %collective-permute-start.14 = (bf16[8,256,128]{2,1,0:T(8,128)(2,1)S(1)}, bf16[8,256,128]{2,1,0:T(8,128)(2,1)S(1)}, u32[]{:S(2)}, u32[]{:S(2)}) collective-permute-start(bf16[8,256,128]{2,1,0:T(8,128)(2,1)S(1)} %shard_map.91.refs_2_), channel_id=1, source_target_pairs={{4,0},{8,4},{12,8},{14,12},{10,14},{6,10},{2,6},{0,2},{1,5},{5,9},... | collective-permute-start | bytes 1572872 | tf_op jit(solution)/shard_map/ppermute | solution.py:290
  67.1 8.1 %collective-permute-start.21 = (bf16[8,256,128]{2,1,0:T(8,128)(2,1)S(1)}, bf16[8,256,128]{2,1,0:T(8,128)(2,1)S(1)}, u32[]{:S(2)}, u32[]{:S(2)}) collective-permute-start(bf16[8,256,128]{2,1,0:T(8,128)(2,1)S(1)} %shard_map.96.refs_2_), channel_id=1, source_target_pairs={{0,1},{1,0},{2,3},{3,2},{4,5},{5,4},{6,7},{7,6},{8,9},{9,8},{10,11... | collective-permute-start | bytes 1572872 | tf_op jit(solution)/shard_map/ppermute | solution.py:293
  67.1 11.0 %collective-permute-start.24 = (bf16[8,256,128]{2,1,0:T(8,128)(2,1)S(1)}, bf16[8,256,128]{2,1,0:T(8,128)(2,1)S(1)}, u32[]{:S(2)}, u32[]{:S(2)}) collective-permute-start(bf16[8,256,128]{2,1,0:T(8,128)(2,1)S(1)} %shard_map.96.refs_2_), channel_id=1, source_target_pairs={{0,4},{4,8},{8,12},{12,14},{14,10},{10,6},{6,2},{2,0},{5,1},{9,5},... | collective-permute-start | bytes 1572872 | tf_op jit(solution)/shard_map/ppermute | solution.py:290
  72.5 7.8 %collective-permute-start.19 = (bf16[8,256,128]{2,1,0:T(8,128)(2,1)S(1)}, bf16[8,256,128]{2,1,0:T(8,128)(2,1)S(1)}, u32[]{:S(2)}, u32[]{:S(2)}) collective-permute-start(bf16[8,256,128]{2,1,0:T(8,128)(2,1)S(1)} %shard_map.95.refs_2_), channel_id=1, source_target_pairs={{0,1},{1,0},{2,3},{3,2},{4,5},{5,4},{6,7},{7,6},{8,9},{9,8},{10,11... | collective-permute-start | bytes 1572872 | tf_op jit(solution)/shard_map/ppermute | solution.py:293
  72.5 11.5 %collective-permute-start.18 = (bf16[8,256,128]{2,1,0:T(8,128)(2,1)S(1)}, bf16[8,256,128]{2,1,0:T(8,128)(2,1)S(1)}, u32[]{:S(2)}, u32[]{:S(2)}) collective-permute-start(bf16[8,256,128]{2,1,0:T(8,128)(2,1)S(1)} %shard_map.95.refs_2_), channel_id=1, source_target_pairs={{4,0},{8,4},{12,8},{14,12},{10,14},{6,10},{2,6},{0,2},{1,5},{5,9},... | collective-permute-start | bytes 1572872 | tf_op jit(solution)/shard_map/ppermute | solution.py:290
  78.2 8.3 %collective-permute-start.25 = (bf16[8,256,128]{2,1,0:T(8,128)(2,1)S(1)}, bf16[8,256,128]{2,1,0:T(8,128)(2,1)S(1)}, u32[]{:S(2)}, u32[]{:S(2)}) collective-permute-start(bf16[8,256,128]{2,1,0:T(8,128)(2,1)S(1)} %shard_map.100.refs_2_), channel_id=1, source_target_pairs={{0,1},{1,0},{2,3},{3,2},{4,5},{5,4},{6,7},{7,6},{8,9},{9,8},{10,11... | collective-permute-start | bytes 1572872 | tf_op jit(solution)/shard_map/ppermute | solution.py:293
  78.7 11.2 %collective-permute-start.27 = (bf16[8,256,128]{2,1,0:T(8,128)(2,1)S(1)}, bf16[8,256,128]{2,1,0:T(8,128)(2,1)S(1)}, u32[]{:S(2)}, u32[]{:S(2)}) collective-permute-start(bf16[8,256,128]{2,1,0:T(8,128)(2,1)S(1)} %shard_map.100.refs_2_), channel_id=1, source_target_pairs={{0,4},{4,8},{8,12},{12,14},{14,10},{10,6},{6,2},{2,0},{5,1},{9,5},... | collective-permute-start | bytes 1572872 | tf_op jit(solution)/shard_map/ppermute | solution.py:290
  84.0 9.6 %collective-permute-start.22 = (bf16[8,256,128]{2,1,0:T(8,128)(2,1)S(1)}, bf16[8,256,128]{2,1,0:T(8,128)(2,1)S(1)}, u32[]{:S(2)}, u32[]{:S(2)}) collective-permute-start(bf16[8,256,128]{2,1,0:T(8,128)(2,1)S(1)} %shard_map.99.refs_2_), channel_id=1, source_target_pairs={{4,0},{8,4},{12,8},{14,12},{10,14},{6,10},{2,6},{0,2},{1,5},{5,9},... | collective-permute-start | bytes 1572872 | tf_op jit(solution)/shard_map/ppermute | solution.py:290
  (16 other events, 102.6 us)

commit v2 on v1

--- a/solution.py
+++ b/solution.py
@@ -9,7 +9,7 @@
 
 THERMAL = 0.3
 SLOTS = 32
-FIRST_SLOTS = 16
+FIRST_SLOTS = 20
 GROUP = 4
 ENTRY_BITS = 5
 
@@ -18,33 +18,16 @@
 ANY = pl.BlockSpec(memory_space=pl.ANY)
 
 
-def stage_body(stage, first, reach, layout, n_pieces, n_extra, *refs):
-    plan_in, dipole = refs[:2]
+def stage_body(stage, first, reach, layout, n_pieces, n_behind, *refs):
+    plan, dipole = refs[:2]
     pieces = refs[2 : 2 + n_pieces]
-    refs = refs[2 + n_pieces + n_extra :]
+    refs = refs[2 + n_pieces + n_behind :]
     if not first:
         refs = refs[2:]
-    moments, entries, _, plan, low, plan_sem, entry_sems, piece_sems = refs
+    moments, entries, _, entry_sems = refs
     n_slots, comps, block, _ = entries.shape
     total, low_bits = layout
-
-    plan_copy = pltpu.make_async_copy(plan_in, plan, plan_sem)
-    plan_copy.start()
-    offset = 0
-    piece_copies = []
-    for i, piece in enumerate(pieces):
-        count = piece.shape[0]
-        piece_copies.append(
-            pltpu.make_async_copy(piece, low.at[pl.ds(offset, count)], piece_sems.at[i])
-        )
-        offset += count
-    for copy in piece_copies:
-        copy.start()
-    if first:
-        moments[...] = jnp.zeros_like(moments)
-    blank = low.shape[0] - 1
-    low[blank] = jnp.zeros(low.shape[1:], low.dtype)
-    plan_copy.wait()
+    low_mask = (1 << low_bits) - 1
 
     begin = plan[total + stage]
     end = plan[total + stage + 1]
@@ -58,20 +41,26 @@
         return pos & (n_slots - 1) if n_slots & (n_slots - 1) == 0 else lax.rem(pos, n_slots)
 
     def row(code):
-        return code >> (low_bits + ENTRY_BITS)
+        return code >> (low_bits + 1 + ENTRY_BITS)
 
     def load(pos):
         code = plan[pos]
         slot = place(pos)
-        entry = (code >> low_bits) & ((1 << ENTRY_BITS) - 1)
+        entry = (code >> (low_bits + 1)) & ((1 << ENTRY_BITS) - 1)
         return pltpu.make_async_copy(dipole.at[row(code), entry], entries.at[slot], entry_sems.at[slot])
 
     @pl.loop(ready, ahead)
     def _(pos):
         load(pos).start()
 
-    for copy in piece_copies:
-        copy.wait()
+    if first:
+        moments[...] = jnp.zeros_like(moments)
+
+    def lower_block(code):
+        index = code & low_mask
+        if len(pieces) == 1:
+            return pieces[0][index]
+        return jnp.where((code >> low_bits) & 1 == 1, pieces[1][index], pieces[0][index])
 
     def work(start):
         positions = [start + i for i in range(GROUP)]
@@ -86,10 +75,10 @@
         kept = [jnp.minimum(pos, end - 1) for pos in positions]
         codes = [plan[pos] for pos in kept]
         rows = [row(code) for code in codes]
-        picks = [
-            jnp.where(pos < end, code & ((1 << low_bits) - 1), blank) for pos, code in zip(positions, codes)
+        blocks = [
+            jnp.where(pos < end, lower_block(code), 0).astype(jnp.bfloat16)
+            for pos, code in zip(positions, codes)
         ]
-        blocks = [low[pick] for pick in picks]
         for a in range(comps):
             products = [
                 jnp.dot(entries[place(pos), a], lower, preferred_element_type=jnp.float32)
@@ -115,12 +104,21 @@
         load(pos).wait()
 
 
-def split_halves(sums, bits, level, keep, send):
+def split_parts(sums, bits, levels, parts):
     comps, count, share, lower_count = sums.shape
-    halves = sums.reshape(comps, count // 2, 2, share, lower_count)
-    side = jnp.broadcast_to(bits[level][None, None, :1], (comps, count // 2, share, lower_count)) > 0
-    keep[...] = jnp.where(side, halves[:, :, 1], halves[:, :, 0])
-    send[...] = jnp.where(side, halves[:, :, 0], halves[:, :, 1])
+    pieces = [sums]
+    for level in levels:
+        side = jnp.broadcast_to(
+            bits[level][None, None, :1], (comps, pieces[0].shape[1] // 2, share, lower_count)
+        ) > 0
+        same, other = [], []
+        for piece in pieces:
+            halves = piece.reshape(comps, piece.shape[1] // 2, 2, share, lower_count)
+            same.append(jnp.where(side, halves[:, :, 1], halves[:, :, 0]))
+            other.append(jnp.where(side, halves[:, :, 0], halves[:, :, 1]))
+        pieces = same + other
+    for piece, part in zip(pieces, parts):
+        part[...] = piece
 
 
 def project(upper_t, moments, comps, lay):
@@ -161,40 +159,55 @@
     share = upper_count // group
     levels = bits.shape[0]
 
-    def shapes(count):
-        return [jax.ShapeDtypeStruct((comps, count, share, lower_count), jnp.float32)] * 2
-
-    def first(upper_t, moments, bits, keep, send):
-        split_halves(project(upper_t, moments, comps, (group, share)), bits, 0, keep, send)
-
-    def middle(level, held, other, bits, keep, send):
-        split_halves(held[...] + other[...], bits, level, keep, send)
-
-    def final(held, other, factor, strength, intensity):
-        own = (held[...] + other[...])[:, 0]
+    rounds = [[0]] + [list(range(i, min(i + 2, levels))) for i in range(1, levels, 2)]
+    left = group
+
+    def shapes(number):
+        count = left >> len(rounds[number])
+        return [jax.ShapeDtypeStruct((comps, count, share, lower_count), jnp.float32)] * (
+            1 << len(rounds[number])
+        )
+
+    def first(upper_t, moments, bits, *parts):
+        split_parts(project(upper_t, moments, comps, (group, share)), bits, rounds[0], parts)
+
+    def middle(number, n_sums, *refs):
+        total = refs[0][...]
+        for ref in refs[1:n_sums]:
+            total = total + ref[...]
+        split_parts(total, refs[n_sums], rounds[number], refs[n_sums + 1 :])
+
+    def final(n_sums, *refs):
+        total = refs[0][...]
+        for ref in refs[1:n_sums]:
+            total = total + ref[...]
+        factor, strength, intensity = refs[n_sums:]
+        own = total[:, 0]
         strength[...] = jnp.sum(own * own, axis=0)
         intensity[...] = factor[...] * strength[...]
 
-    keep, send = small_call(first, shapes(group // 2), upper_t, moments, bits)
-    for level in range(levels):
-        bit = 1 << level
-        other = lax.ppermute(send, "blk", [(d, d ^ bit) for d in range(group)])
-        if level + 1 < levels:
-            count = group >> (level + 2)
-            keep, send = small_call(
-                functools.partial(middle, level + 1), shapes(count), keep, other, bits
+    parts = small_call(first, shapes(0), upper_t, moments, bits)
+    for number, used in enumerate(rounds):
+        left >>= len(used)
+        terms = [parts[0]]
+        for choice in range(1, len(parts)):
+            mask = sum(1 << level for i, level in enumerate(used) if (choice >> i) & 1)
+            terms.append(lax.ppermute(parts[choice], "blk", [(d, d ^ mask) for d in range(group)]))
+        if number + 1 < len(rounds):
+            parts = small_call(
+                functools.partial(middle, number + 1, len(terms)), shapes(number + 1), *terms, bits
             )
     out = [jax.ShapeDtypeStruct((share, lower_count), jnp.float32)] * 2
-    return small_call(final, out, keep, other, factor)
-
-
-def run_stage(stage, reach, plan, layout, dipole, pieces, lower_count, state, needed=()):
+    return small_call(functools.partial(final, len(terms)), out, *terms, factor)
+
+
+def run_stage(stage, reach, plan, layout, dipole, pieces, lower_count, state, behind=()):
     rows, _, comps, block, _ = dipole.shape
     first = state is None
-    low_blocks = sum(p.shape[0] for p in pieces) + 1
+    low_blocks = sum(p.shape[0] for p in pieces)
     n_slots = min(SLOTS, layout[0])
-    operands = [plan, dipole, *pieces, *needed]
-    in_specs = [ANY] * len(operands)
+    operands = [plan, dipole, *pieces, *behind]
+    in_specs = [SMEM, ANY] + [VMEM] * len(pieces) + [ANY] * len(behind)
     aliases = {}
     if not first:
         aliases = {len(operands): 0, len(operands) + 1: 1}
@@ -202,7 +215,7 @@
         in_specs += [VMEM, VMEM]
     entries = layout[0] / 16
     result = pl.pallas_call(
-        functools.partial(stage_body, stage, first, reach, layout, len(pieces), len(needed)),
+        functools.partial(stage_body, stage, first, reach, layout, len(pieces), len(behind)),
         out_shape=[
             pltpu.VMEM((rows, comps * block, lower_count), jnp.float32),
             pltpu.VMEM((n_slots, comps, block, block), jnp.bfloat16),
@@ -212,31 +225,58 @@
         out_specs=[VMEM, VMEM, ANY],
         input_output_aliases=aliases,
         scratch_shapes=[
-            pltpu.SMEM(plan.shape, jnp.int32),
-            pltpu.VMEM((low_blocks, block, lower_count), jnp.bfloat16),
-            pltpu.SemaphoreType.DMA,
             pltpu.SemaphoreType.DMA((n_slots,)),
-            pltpu.SemaphoreType.DMA((max(len(pieces), 1),)),
         ],
         cost_estimate=pl.CostEstimate(
             flops=int(entries * comps * block * block * lower_count * 2),
             bytes_accessed=int(entries * comps * block * block * 2),
             transcendentals=0,
         ),
-        compiler_params=pltpu.CompilerParams(vmem_limit_bytes=(8 if low_blocks < 64 else 30) * 2**20),
+        compiler_params=pltpu.CompilerParams(vmem_limit_bytes=(8 if low_blocks < 64 else 40) * 2**20),
     )(*operands)
     return result[:2], result[2]
 
 
-def after(done, array):
+def after(done, *arrays):
+    count = len(arrays)
     return pl.pallas_call(
         lambda *refs: None,
-        out_shape=jax.ShapeDtypeStruct(array.shape, array.dtype),
-        in_specs=[ANY, ANY],
+        out_shape=[jax.ShapeDtypeStruct(x.shape, x.dtype) for x in arrays],
+        in_specs=[ANY] * (count + 1),
+        out_specs=[ANY] * count,
+        input_output_aliases={i: i for i in range(count)},
+        compiler_params=pltpu.CompilerParams(has_side_effects=True, vmem_limit_bytes=2**20),
+    )(*arrays, done)
+
+
+def transposed(array, behind):
+    rows, columns = array.shape
+    step = min(rows, columns)
+
+    def body(source, _, target):
+        for i in range(0, rows, step):
+            target[:, pl.ds(i, step)] = source[pl.ds(i, step), :].T
+
+    return pl.pallas_call(
+        body,
+        out_shape=jax.ShapeDtypeStruct((columns, rows), array.dtype),
+        in_specs=[VMEM, ANY],
+        out_specs=VMEM,
+        compiler_params=pltpu.CompilerParams(vmem_limit_bytes=8 * 2**20),
+    )(array, behind)
+
+
+def part_of(array, start, count, *needed):
+    def body(*refs):
+        pltpu.sync_copy(refs[0].at[pl.ds(start, count)], refs[-1])
+
+    return pl.pallas_call(
+        body,
+        out_shape=jax.ShapeDtypeStruct((count,) + array.shape[1:], array.dtype),
+        in_specs=[pl.BlockSpec(memory_space=pltpu.HBM)] + [SMEM] * len(needed),
         out_specs=ANY,
-        input_output_aliases={0: 0},
-        compiler_params=pltpu.CompilerParams(has_side_effects=True, vmem_limit_bytes=2**20),
-    )(array, done)
+        compiler_params=pltpu.CompilerParams(vmem_limit_bytes=2**20),
+    )(array, *needed)
 
 
 def sorted_entries(stage, slot, n_stages, low_bits):
@@ -244,17 +284,23 @@
     total = rows * count
     row = lax.broadcasted_iota(jnp.int32, stage.shape, 0)
     entry = lax.broadcasted_iota(jnp.int32, stage.shape, 1)
-    code = ((((row << ENTRY_BITS) + entry) << low_bits) + slot).reshape(total)
+    code = ((((row << ENTRY_BITS) + entry) << (low_bits + 1)) + slot).reshape(total)
     key = (stage * total + row * count + entry).reshape(total)
     rank = jnp.sum((key[None, :] < key[:, None]).astype(jnp.int32), axis=1)
     length = -(-(total + n_stages + 1) // 128) * 128
     place = jnp.arange(length, dtype=jnp.int32)
     codes = jnp.sum(jnp.where(rank[:, None] == place[None, :], code[:, None], 0), axis=0)
     bounds = jnp.sum((stage.reshape(total, 1) < place[None, :] - total).astype(jnp.int32), axis=0)
-    return jnp.where(place < total, codes, bounds)
-
-
-def ring_moments(dipole, block_cols, lower_blocks, group, needed):
+    return pl.pallas_call(
+        lambda source, plan: pltpu.sync_copy(source, plan),
+        out_shape=pltpu.SMEM((length,), jnp.int32),
+        in_specs=[ANY],
+        out_specs=SMEM,
+        compiler_params=pltpu.CompilerParams(vmem_limit_bytes=2**20),
+    )(jnp.where(place < total, codes, bounds))
+
+
+def ring_moments(dipole, block_cols, lower_blocks, upper_vecs, group, needed):
     rows = dipole.shape[0]
     lower_count = lower_blocks.shape[2]
     me = lax.axis_index("blk")
@@ -279,35 +325,42 @@
     mine, theirs = position(me), position(owner)
     hops = jnp.where(forward, mine - theirs, theirs - mine) % chips
     other_core = (owner + me) % 2
-    stage = jnp.where(hops == 0, 1, 2 * hops + part)
-    slot = jnp.where(hops == 0, other_core * rows + local, other_core * half + local % half)
-    n_stages = 2 * chips
-    layout = (block_cols.size, (2 * rows - 1).bit_length())
-    plan = sorted_entries(stage, slot, n_stages, layout[1])
+    stage = 1 + jnp.where(hops == 0, other_core, 2 * hops + part)
+    index = jnp.where(hops == 0, local, local % half)
+    n_stages = 2 * chips + 1
+    layout = (block_cols.size, (rows - 1).bit_length())
+    plan = sorted_entries(stage, (other_core << layout[1]) + index, n_stages, layout[1])
     reach = [FIRST_SLOTS] + [SLOTS] * (n_stages - 1)
 
     def hop(array, p):
         return lax.ppermute(array, "blk", ways[p])
 
     def cross(array):
-        return [array, lax.ppermute(array, "blk", sibling)]
-
-    def compute(number, arrived, state, needed=()):
-        return run_stage(number, reach, plan, layout, dipole, arrived, lower_count, state, needed)
-
-    flying = [hop(lower_blocks[p * half : (p + 1) * half], p) for p in range(2)]
-    waiting = (1, cross(lower_blocks))
-    state, done = compute(0, [], None, needed)
+        return lax.ppermute(array, "blk", sibling)
+
+    def compute(number, arrived, state, *behind):
+        return run_stage(number, reach, plan, layout, dipole, arrived, lower_count, state, behind)
+
+    flying = [hop(part_of(lower_blocks, 0, half), 0)]
+    there = cross(lower_blocks)
+    second = part_of(lower_blocks, half, half, plan)
+    flying.append(hop(second, 1))
+    waiting = [(1, [lower_blocks]), (2, [there])]
+    state, done = compute(0, [], None, second, *needed)
+    upper_t = None
     for h in range(1, chips):
         for p in range(2):
-            here = after(done, flying[p])
+            here = after(done, flying[p])[0]
             if h < chips - 1:
                 flying[p] = hop(here, p)
-            here = cross(here)
-            state, done = compute(*waiting, state)
-            waiting = (2 * h + p, here)
-    state, done = compute(*waiting, state)
-    return state[0]
+            waiting.append((2 * h + p + 1, [here, cross(here)]))
+            for _ in range(2 if (h, p) == (1, 0) else 1):
+                state, done = compute(*waiting.pop(0), state, here)
+            if upper_t is None and 2 * h >= chips:
+                done = upper_t = transposed(upper_vecs, done)
+    for number, arrived in waiting:
+        state, done = compute(number, arrived, state)
+    return state[0], upper_t
 
 
 def gathered_moments(dipole, block_cols, lower_blocks):
@@ -339,7 +392,6 @@
     group = lax.axis_size("blk")
     me = lax.axis_index("blk")
     lower_blocks = lower_vecs.reshape(rows, block, lower_vecs.shape[1])
-    upper_t = upper_vecs.T
     share = upper_vecs.shape[1] // group
     energy = lax.dynamic_slice_in_dim(upper_energy, me * share, share, 0)
     wavenumber = energy[:, None] - lower_energy[None, :]
@@ -348,10 +400,12 @@
     if rows % 2 == 0 and share % 8 == 0 and group >= 8 and group & (group - 1) == 0:
         levels = jnp.arange(group.bit_length() - 1, dtype=jnp.int32)
         bits = jnp.broadcast_to(((me >> levels) & 1)[:, None, None], (levels.shape[0], 8, 128))
-        needed = [upper_t, factor, bits]
-        moments = ring_moments(dipole, block_cols, lower_blocks, group, needed)
+        moments, upper_t = ring_moments(
+            dipole, block_cols, lower_blocks, upper_vecs, group, [factor, bits]
+        )
         return own_outputs(upper_t, moments, comps, bits, factor, group)
     moments = gathered_moments(dipole, block_cols, lower_blocks)
+    upper_t = upper_vecs.T
 
     def body(upper_t, moments, proj):
         proj[...] = project(upper_t, moments, comps, (upper_t.shape[0],))

time: 119 us -> 114 us (0.958)
  Pallas kernels: 59.2 us -> 49.8 us
  waiting for transfers between devices: 13.7 us -> 18.3 us
  local copies, waits for them, and re-layouts: 5.6 us -> 3.82 us
  other arithmetic: 1.99 us -> 3.3 us
    pallas_call x16 -> x17, Pallas kernels: 56.7 us -> 46.1 us  [run_stage(): pl.pallas_call(functools.partial(stage_body, stage, first, reach, layout,...]
    ppermute x14, waiting for transfers between devices: 4.21 us -> 9.06 us  [hop(): return lax.ppermute(array, 'blk', ways[p])]
    ppermute x19 -> x20, starting transfers between devices: 9.59 us -> 12.3 us  [the longest x5 7.17 us: own_outputs(): lax.ppermute(parts[choice], 'blk', [(d, d ^ mask) for d in range(group)])]
    ppermute x14, starting transfers between devices: 27.3 us -> 25 us  [hop(): return lax.ppermute(array, 'blk', ways[p])]
    slice x1 -> x0, local copies, waits for them, and re-layouts: 2.24 us -> none  [ring_moments(): flying = [hop(lower_blocks[p * half:(p + 1) * half], p) for p in range(2)]]
    pallas_call x14 -> x18, Pallas kernels: 0.02 us -> 1.27 us  [the longest x1 0.62 us: transposed(): pl.pallas_call(body, out_shape=jax.ShapeDtypeStruct((columns, rows), arra...]
    ppermute x19 -> x20, waiting for transfers between devices: 9.5 us -> 9.25 us  [the longest x5 9.21 us: own_outputs(): lax.ppermute(parts[choice], 'blk', [(d, d ^ mask) for d in range(group)])]
    unnamed x15 -> x16, local copies, waits for them, and re-layouts: 2.95 us -> 2.74 us
  transfers between devices with their start and end apart: 33 -> 34, of which waited for: 9 -> 12; matrix products, arithmetic and copies ran while one was open for 6% -> 4% of each run, Pallas kernels for 45% -> 39%
where the time goes in v2:
time: 114 us
  Pallas kernels  49.8 us (44%)
  starting transfers between devices  37.3 us (33%)
  waiting for transfers between devices  18.3 us (16%)
  local copies, waits for them, and re-layouts  3.82 us (3%)
  other arithmetic  3.3 us (3%)
    pallas_call x17, Pallas kernels, run_stage(): pl.pallas_call(functools.partial(stage_body, stage, first, reach, layout,...  46.1 us
    ppermute x14, starting transfers between devices, hop(): return lax.ppermute(array, 'blk', ways[p])  25 us
    ppermute x5, waiting for transfers between devices, own_outputs(): lax.ppermute(parts[choice], 'blk', [(d, d ^ mask) for d in range(group)])  9.21 us
    ppermute x14, waiting for transfers between devices, hop(): return lax.ppermute(array, 'blk', ways[p])  9.06 us
    ppermute x5, starting transfers between devices, own_outputs(): lax.ppermute(parts[choice], 'blk', [(d, d ^ mask) for d in range(group)])  7.17 us
    ppermute x15, starting transfers between devices, cross(): return lax.ppermute(array, 'blk', sibling)  5.1 us
    unnamed x16, local copies, waits for them, and re-layouts  2.74 us
    pallas_call x4, Pallas kernels, small_call(): pl.pallas_call(body, out_shape=out_shape, in_specs=[VMEM] * len(operands)...  2.45 us
  transfers between devices with their start and end apart: 34, of which 12 were waited for; matrix products, arithmetic and copies ran while one was open for 4% of the time, Pallas kernels for 39%

profile of v2, /device:TPU:0, one launch (start us, length us, event | category | flops | bytes accessed | tf_op | source)
XLA Modules:
  0.0 113.6 jit_solution(14034667148519065013)
XLA Ops:
  2.4 2.6 %collective-permute-start.2 = (bf16[8,256,128]{2,1,0:T(8,128)(2,1)S(1)}, bf16[8,256,128]{2,1,0:T(8,128)(2,1)S(1)}, u32[]{:S(2)}, u32[]{:S(2)}) collective-permute-start(bf16[8,256,128]{2,1,0:T(8,128)(2,1)S(1)} %shard_map.79), channel_id=1, source_target_pairs={{0,4},{4,8},{8,12},{12,14},{14,10},{10,6},{6,2},{2,0},{5,1},{9,5},... | collective-permute-start | bytes 1572872 | tf_op jit(solution)/shard_map/ppermute | solution.py:336
  11.4 3.6 %shard_map.80 = (f32[16,768,128]{2,1,0:T(8,128)S(1)}, bf16[32,3,256,256]{3,2,1,0:T(8,128)(2,1)S(1)}, f32[8,128]{1,0:T(8,128)S(1)}) custom-call(s32[256]{0:T(256)S(4)} %shard_map.77.refs_1_.refs_0_, bf16[16,12,3,256,256]{4,3,2,1,0:T(8,128)(2,1)} %refs_1_.33, bf16[8,256,128]{2,1,0:T(8,128)(2,1)S(1)} %shard_map.78.refs_2_, ...), custom_call_target="tpu_custom_call" | custom-call | flops 603979776 | bytes 4718592 | tf_op jit(solution)/shard_map/pallas_call | solution.py:217
  17.2 2.8 %shard_map.82 = (f32[16,768,128]{2,1,0:T(8,128)S(1)}, bf16[32,3,256,256]{3,2,1,0:T(8,128)(2,1)S(1)}, f32[8,128]{1,0:T(8,128)}) custom-call(s32[256]{0:T(256)S(4)} %shard_map.77.refs_1_.refs_0_, bf16[16,12,3,256,256]{4,3,2,1,0:T(8,128)(2,1)} %refs_1_.33, bf16[16,256,128]{2,1,0:T(8,128)(2,1)S(1)} %bitcast.4, ...), custom_call_target="tpu_custom_call", output_to_operand_aliasing={{0}: (4, {}), {1}: (5, {})} | custom-call | flops 603979776 | bytes 4718592 | tf_op jit(solution)/shard_map/pallas_call | solution.py:217
  20.0 3.1 %shard_map.83 = (f32[16,768,128]{2,1,0:T(8,128)S(1)}, bf16[32,3,256,256]{3,2,1,0:T(8,128)(2,1)S(1)}, f32[8,128]{1,0:T(8,128)S(1)}) custom-call(s32[256]{0:T(256)S(4)} %shard_map.77.refs_1_.refs_0_, bf16[16,12,3,256,256]{4,3,2,1,0:T(8,128)(2,1)} %refs_1_.33, ...), custom_call_target="tpu_custom_call", output_to_operand_aliasing={{0}: (4, {}), {1}: (5, {})} | custom-call | flops 603979776 | bytes 4718592 | tf_op jit(solution)/shard_map/pallas_call | solution.py:217
  24.9 2.5 %shard_map.85 = (f32[16,768,128]{2,1,0:T(8,128)S(1)}, bf16[32,3,256,256]{3,2,1,0:T(8,128)(2,1)S(1)}, f32[8,128]{1,0:T(8,128)S(1)}) custom-call(s32[256]{0:T(256)S(4)} %shard_map.77.refs_1_.refs_0_, bf16[16,12,3,256,256]{4,3,2,1,0:T(8,128)(2,1)} %refs_1_.33, ...), custom_call_target="tpu_custom_call", output_to_operand_aliasing={{0}: (5, {}), {1}: (6, {})} | custom-call | flops 603979776 | bytes 4718592 | tf_op jit(solution)/shard_map/pallas_call | solution.py:217
  29.6 2.2 %shard_map.87 = (f32[16,768,128]{2,1,0:T(8,128)S(1)}, bf16[32,3,256,256]{3,2,1,0:T(8,128)(2,1)S(1)}, f32[8,128]{1,0:T(8,128)S(1)}) custom-call(s32[256]{0:T(256)S(4)} %shard_map.77.refs_1_.refs_0_, bf16[16,12,3,256,256]{4,3,2,1,0:T(8,128)(2,1)} %refs_1_.33, ...), custom_call_target="tpu_custom_call", output_to_operand_aliasing={{0}: (5, {}), {1}: (6, {})} | custom-call | flops 603979776 | bytes 4718592 | tf_op jit(solution)/shard_map/pallas_call | solution.py:217
  31.8 2.5 %collective-permute-done.3.refs_0_ = bf16[8,256,128]{2,1,0:T(8,128)(2,1)S(1)} collective-permute-done((bf16[8,256,128]{2,1,0:T(8,128)(2,1)S(1)}, bf16[8,256,128]{2,1,0:T(8,128)(2,1)S(1)}, u32[]{:S(2)}, u32[]{:S(2)}) %collective-permute-start.3) | collective-permute-done | bytes 524320 | tf_op jit(solution)/shard_map/ppermute | solution.py:336
  35.4 2.6 %shard_map.89 = (f32[16,768,128]{2,1,0:T(8,128)S(1)}, bf16[32,3,256,256]{3,2,1,0:T(8,128)(2,1)S(1)}, f32[8,128]{1,0:T(8,128)S(1)}) custom-call(s32[256]{0:T(256)S(4)} %shard_map.77.refs_1_.refs_0_, bf16[16,12,3,256,256]{4,3,2,1,0:T(8,128)(2,1)} %refs_1_.33, ...), custom_call_target="tpu_custom_call", output_to_operand_aliasing={{0}: (5, {}), {1}: (6, {})} | custom-call | flops 603979776 | bytes 4718592 | tf_op jit(solution)/shard_map/pallas_call | solution.py:217
  41.1 2.3 %shard_map.91 = (f32[16,768,128]{2,1,0:T(8,128)S(1)}, bf16[32,3,256,256]{3,2,1,0:T(8,128)(2,1)S(1)}, f32[8,128]{1,0:T(8,128)S(1)}) custom-call(s32[256]{0:T(256)S(4)} %shard_map.77.refs_1_.refs_0_, bf16[16,12,3,256,256]{4,3,2,1,0:T(8,128)(2,1)} %refs_1_.33, ...), custom_call_target="tpu_custom_call", output_to_operand_aliasing={{0}: (5, {}), {1}: (6, {})} | custom-call | flops 603979776 | bytes 4718592 | tf_op jit(solution)/shard_map/pallas_call | solution.py:217
  45.3 2.2 %collective-permute-start.14 = (bf16[8,256,128]{2,1,0:T(8,128)(2,1)S(1)}, bf16[8,256,128]{2,1,0:T(8,128)(2,1)S(1)}, u32[]{:S(2)}, u32[]{:S(2)}) collective-permute-start(bf16[8,256,128]{2,1,0:T(8,128)(2,1)S(1)} %shard_map.92.refs_4_.refs_2_), channel_id=1, source_target_pairs={{4,0},{8,4},{12,8},{14,12},{10,14},{6,10},{2,6},{0,2},{1,5},{5,9},... | collective-permute-start | bytes 1572872 | tf_op jit(solution)/shard_map/ppermute | solution.py:336
  47.5 2.5 %shard_map.93 = (f32[16,768,128]{2,1,0:T(8,128)S(1)}, bf16[32,3,256,256]{3,2,1,0:T(8,128)(2,1)S(1)}, f32[8,128]{1,0:T(8,128)S(1)}) custom-call(s32[256]{0:T(256)S(4)} %shard_map.77.refs_1_.refs_0_, bf16[16,12,3,256,256]{4,3,2,1,0:T(8,128)(2,1)} %refs_1_.33, ...), custom_call_target="tpu_custom_call", output_to_operand_aliasing={{0}: (5, {}), {1}: (6, {})} | custom-call | flops 603979776 | bytes 4718592 | tf_op jit(solution)/shard_map/pallas_call | solution.py:217
  51.9 2.6 %shard_map.95 = (f32[16,768,128]{2,1,0:T(8,128)S(1)}, bf16[32,3,256,256]{3,2,1,0:T(8,128)(2,1)S(1)}, f32[8,128]{1,0:T(8,128)S(1)}) custom-call(s32[256]{0:T(256)S(4)} %shard_map.77.refs_1_.refs_0_, bf16[16,12,3,256,256]{4,3,2,1,0:T(8,128)(2,1)} %refs_1_.33, ...), custom_call_target="tpu_custom_call", output_to_operand_aliasing={{0}: (5, {}), {1}: (6, {})} | custom-call | flops 603979776 | bytes 4718592 | tf_op jit(solution)/shard_map/pallas_call | solution.py:217
  58.6 2.2 %shard_map.98 = (f32[16,768,128]{2,1,0:T(8,128)S(1)}, bf16[32,3,256,256]{3,2,1,0:T(8,128)(2,1)S(1)}, f32[8,128]{1,0:T(8,128)S(1)}) custom-call(s32[256]{0:T(256)S(4)} %shard_map.77.refs_1_.refs_0_, bf16[16,12,3,256,256]{4,3,2,1,0:T(8,128)(2,1)} %refs_1_.33, ...), custom_call_target="tpu_custom_call", output_to_operand_aliasing={{0}: (5, {}), {1}: (6, {})} | custom-call | flops 603979776 | bytes 4718592 | tf_op jit(solution)/shard_map/pallas_call | solution.py:217
  63.6 2.9 %shard_map.100 = (f32[16,768,128]{2,1,0:T(8,128)S(1)}, bf16[32,3,256,256]{3,2,1,0:T(8,128)(2,1)S(1)}, f32[8,128]{1,0:T(8,128)S(1)}) custom-call(s32[256]{0:T(256)S(4)} %shard_map.77.refs_1_.refs_0_, bf16[16,12,3,256,256]{4,3,2,1,0:T(8,128)(2,1)} %refs_1_.33, ...), custom_call_target="tpu_custom_call", output_to_operand_aliasing={{0}: (5, {}), {1}: (6, {})} | custom-call | flops 603979776 | bytes 4718592 | tf_op jit(solution)/shard_map/pallas_call | solution.py:217
  67.6 2.5 %collective-permute-start.19 = (bf16[8,256,128]{2,1,0:T(8,128)(2,1)S(1)}, bf16[8,256,128]{2,1,0:T(8,128)(2,1)S(1)}, u32[]{:S(2)}, u32[]{:S(2)}) collective-permute-start(bf16[8,256,128]{2,1,0:T(8,128)(2,1)S(1)} %shard_map.101.refs_4_.refs_2_), channel_id=1, source_target_pairs={{4,0},{8,4},{12,8},{14,12},{10,14},{6,10},{2,6},{0,2},{1,5},{5,9},... | collective-permute-start | bytes 1572872 | tf_op jit(solution)/shard_map/ppermute | solution.py:336
  70.2 3.0 %shard_map.102 = (f32[16,768,128]{2,1,0:T(8,128)S(1)}, bf16[32,3,256,256]{3,2,1,0:T(8,128)(2,1)S(1)}, f32[8,128]{1,0:T(8,128)S(1)}) custom-call(s32[256]{0:T(256)S(4)} %shard_map.77.refs_1_.refs_0_, bf16[16,12,3,256,256]{4,3,2,1,0:T(8,128)(2,1)} %refs_1_.33, ...), custom_call_target="tpu_custom_call", output_to_operand_aliasing={{0}: (5, {}), {1}: (6, {})} | custom-call | flops 603979776 | bytes 4718592 | tf_op jit(solution)/shard_map/pallas_call | solution.py:217
  75.1 3.1 %shard_map.104 = (f32[16,768,128]{2,1,0:T(8,128)S(1)}, bf16[32,3,256,256]{3,2,1,0:T(8,128)(2,1)S(1)}, f32[8,128]{1,0:T(8,128)S(1)}) custom-call(s32[256]{0:T(256)S(4)} %shard_map.77.refs_1_.refs_0_, bf16[16,12,3,256,256]{4,3,2,1,0:T(8,128)(2,1)} %refs_1_.33, ...), custom_call_target="tpu_custom_call", output_to_operand_aliasing={{0}: (5, {}), {1}: (6, {})} | custom-call | flops 603979776 | bytes 4718592 | tf_op jit(solution)/shard_map/pallas_call | solution.py:217
  81.2 2.6 %shard_map.106 = (f32[16,768,128]{2,1,0:T(8,128)S(1)}, bf16[32,3,256,256]{3,2,1,0:T(8,128)(2,1)S(1)}, f32[8,128]{1,0:T(8,128)S(1)}) custom-call(s32[256]{0:T(256)S(4)} %shard_map.77.refs_1_.refs_0_, bf16[16,12,3,256,256]{4,3,2,1,0:T(8,128)(2,1)} %refs_1_.33, ...), custom_call_target="tpu_custom_call", output_to_operand_aliasing={{0}: (5, {}), {1}: (6, {})} | custom-call | flops 603979776 | bytes 4718592 | tf_op jit(solution)/shard_map/pallas_call | solution.py:217
  85.2 2.9 %shard_map.108 = (f32[16,768,128]{2,1,0:T(8,128)S(1)}, bf16[32,3,256,256]{3,2,1,0:T(8,128)(2,1)S(1)}, f32[8,128]{1,0:T(8,128)S(1)}) custom-call(s32[256]{0:T(256)S(4)} %shard_map.77.refs_1_.refs_0_, bf16[16,12,3,256,256]{4,3,2,1,0:T(8,128)(2,1)} %refs_1_.33, ...), custom_call_target="tpu_custom_call", output_to_operand_aliasing={{0}: (5, {}), {1}: (6, {})} | custom-call | flops 603979776 | bytes 4718592 | tf_op jit(solution)/shard_map/pallas_call | solution.py:217
  89.5 2.3 %shard_map.110 = (f32[16,768,128]{2,1,0:T(8,128)S(1)}, bf16[32,3,256,256]{3,2,1,0:T(8,128)(2,1)S(1)}, f32[8,128]{1,0:T(8,128)}) custom-call(s32[256]{0:T(256)S(4)} %shard_map.77.refs_1_.refs_0_, bf16[16,12,3,256,256]{4,3,2,1,0:T(8,128)(2,1)} %refs_1_.33, ...), custom_call_target="tpu_custom_call", output_to_operand_aliasing={{0}: (5, {}), {1}: (6, {})} | custom-call | flops 603979776 | bytes 4718592 | tf_op jit(solution)/shard_map/pallas_call | solution.py:217
  91.9 2.9 %shard_map.111 = (f32[16,768,128]{2,1,0:T(8,128)S(1)}, bf16[32,3,256,256]{3,2,1,0:T(8,128)(2,1)S(1)}, f32[8,128]{1,0:T(8,128)}) custom-call(s32[256]{0:T(256)S(4)} %shard_map.77.refs_1_.refs_0_, bf16[16,12,3,256,256]{4,3,2,1,0:T(8,128)(2,1)} %refs_1_.33, ...), custom_call_target="tpu_custom_call", output_to_operand_aliasing={{0}: (4, {}), {1}: (5, {})} | custom-call | flops 603979776 | bytes 4718592 | tf_op jit(solution)/shard_map/pallas_call | solution.py:217
  98.1 3.2 %collective-permute-start.30 = (f32[3,2,16,128]{3,2,1,0:T(8,128)S(1)}, f32[3,2,16,128]{3,2,1,0:T(8,128)S(1)}, u32[]{:S(2)}, u32[]{:S(2)}) collective-permute-start(f32[3,2,16,128]{3,2,1,0:T(8,128)S(1)} %get-tuple-element.107), channel_id=1, source_target_pairs={{0,2},{1,3},{2,0},{3,1},{4,6},{5,7},{6,4},{7,5},{8,10},{9,11},{10,... | collective-permute-start | bytes 147464 | tf_op jit(solution)/shard_map/ppermute | solution.py:195
  105.5 2.6 %collective-permute-done.32.refs_3_ = f32[3,2,16,128]{3,2,1,0:T(8,128)S(1)} collective-permute-done((f32[3,2,16,128]{3,2,1,0:T(8,128)S(1)}, f32[3,2,16,128]{3,2,1,0:T(8,128)S(1)}, u32[]{:S(2)}, u32[]{:S(2)}) %collective-permute-start.32) | collective-permute-done | bytes 49184 | tf_op jit(solution)/shard_map/ppermute | solution.py:195
  110.2 2.8 %collective-permute-done.33.refs_1_ = f32[3,1,16,128]{3,2,1,0:T(8,128)S(1)} collective-permute-done((f32[3,1,16,128]{3,2,1,0:T(8,128)S(1)}, f32[3,1,16,128]{3,2,1,0:T(8,128)S(1)}, u32[]{:S(2)}, u32[]{:S(2)}) %collective-permute-start.33) | collective-permute-done | bytes 24608 | tf_op jit(solution)/shard_map/ppermute | solution.py:195
  (115 shorter events, 47.9 us)
Async XLA Ops:
  0.6 19.3 %collective-permute-start.1 = (bf16[16,256,128]{2,1,0:T(8,128)(2,1)}, bf16[16,256,128]{2,1,0:T(8,128)(2,1)S(1)}, u32[]{:S(2)}, u32[]{:S(2)}) collective-permute-start(bf16[16,256,128]{2,1,0:T(8,128)(2,1)} %bitcast.1), channel_id=1, source_target_pairs={{0,1},{1,0},{2,3},{3,2},{4,5},{5,4},{6,7},{7,6},{8,9},{9,8},{10,11... | collective-permute-start | bytes 3145736 | tf_op jit(solution)/shard_map/ppermute | solution.py:339
  2.4 12.6 %collective-permute-start.2 = (bf16[8,256,128]{2,1,0:T(8,128)(2,1)S(1)}, bf16[8,256,128]{2,1,0:T(8,128)(2,1)S(1)}, u32[]{:S(2)}, u32[]{:S(2)}) collective-permute-start(bf16[8,256,128]{2,1,0:T(8,128)(2,1)S(1)} %shard_map.79), channel_id=1, source_target_pairs={{0,4},{4,8},{8,12},{12,14},{14,10},{10,6},{6,2},{2,0},{5,1},{9,5},... | collective-permute-start | bytes 1572872 | tf_op jit(solution)/shard_map/ppermute | solution.py:336
  9.1 14.0 %collective-permute-start = (bf16[8,256,128]{2,1,0:T(8,128)(2,1)S(1)}, bf16[8,256,128]{2,1,0:T(8,128)(2,1)S(1)}, u32[]{:S(2)}, u32[]{:S(2)}) collective-permute-start(bf16[8,256,128]{2,1,0:T(8,128)(2,1)S(1)} %shard_map.78.refs_2_), channel_id=1, source_target_pairs={{4,0},{8,4},{12,8},{14,12},{10,14},{6,10},{2,6},{0,2},{1,5},{5,9},... | collective-permute-start | bytes 1572872 | tf_op jit(solution)/shard_map/ppermute | solution.py:336
  15.0 9.8 %collective-permute-start.6 = (bf16[8,256,128]{2,1,0:T(8,128)(2,1)S(1)}, bf16[8,256,128]{2,1,0:T(8,128)(2,1)S(1)}, u32[]{:S(2)}, u32[]{:S(2)}) collective-permute-start(bf16[8,256,128]{2,1,0:T(8,128)(2,1)S(1)} %shard_map.81.refs_3_.refs_2_), channel_id=1, source_target_pairs={{0,1},{1,0},{2,3},{3,2},{4,5},{5,4},{6,7},{7,6},{8,9},{9,8},{10,11... | collective-permute-start | bytes 1572872 | tf_op jit(solution)/shard_map/ppermute | solution.py:339
  15.4 12.0 %collective-permute-start.5 = (bf16[8,256,128]{2,1,0:T(8,128)(2,1)S(1)}, bf16[8,256,128]{2,1,0:T(8,128)(2,1)S(1)}, u32[]{:S(2)}, u32[]{:S(2)}) collective-permute-start(bf16[8,256,128]{2,1,0:T(8,128)(2,1)S(1)} %shard_map.81.refs_3_.refs_2_), channel_id=1, source_target_pairs={{0,4},{4,8},{8,12},{12,14},{14,10},{10,6},{6,2},{2,0},{5,1},{9,5},... | collective-permute-start | bytes 1572872 | tf_op jit(solution)/shard_map/ppermute | solution.py:336
  23.3 11.1 %collective-permute-start.3 = (bf16[8,256,128]{2,1,0:T(8,128)(2,1)S(1)}, bf16[8,256,128]{2,1,0:T(8,128)(2,1)S(1)}, u32[]{:S(2)}, u32[]{:S(2)}) collective-permute-start(bf16[8,256,128]{2,1,0:T(8,128)(2,1)S(1)} %shard_map.84.refs_4_.refs_2_), channel_id=1, source_target_pairs={{4,0},{8,4},{12,8},{14,12},{10,14},{6,10},{2,6},{0,2},{1,5},{5,9},... | collective-permute-start | bytes 1572872 | tf_op jit(solution)/shard_map/ppermute | solution.py:336
  27.4 8.1 %collective-permute-start.10 = (bf16[8,256,128]{2,1,0:T(8,128)(2,1)S(1)}, bf16[8,256,128]{2,1,0:T(8,128)(2,1)S(1)}, u32[]{:S(2)}, u32[]{:S(2)}) collective-permute-start(bf16[8,256,128]{2,1,0:T(8,128)(2,1)S(1)} %shard_map.86.refs_4_.refs_2_), channel_id=1, source_target_pairs={{0,1},{1,0},{2,3},{3,2},{4,5},{5,4},{6,7},{7,6},{8,9},{9,8},{10,11... | collective-permute-start | bytes 1572872 | tf_op jit(solution)/shard_map/ppermute | solution.py:339
  27.7 10.4 %collective-permute-start.9 = (bf16[8,256,128]{2,1,0:T(8,128)(2,1)S(1)}, bf16[8,256,128]{2,1,0:T(8,128)(2,1)S(1)}, u32[]{:S(2)}, u32[]{:S(2)}) collective-permute-start(bf16[8,256,128]{2,1,0:T(8,128)(2,1)S(1)} %shard_map.86.refs_4_.refs_2_), channel_id=1, source_target_pairs={{0,4},{4,8},{8,12},{12,14},{14,10},{10,6},{6,2},{2,0},{5,1},{9,5},... | collective-permute-start | bytes 1572872 | tf_op jit(solution)/shard_map/ppermute | solution.py:336
  34.3 6.7 %collective-permute-start.8 = (bf16[8,256,128]{2,1,0:T(8,128)(2,1)S(1)}, bf16[8,256,128]{2,1,0:T(8,128)(2,1)S(1)}, u32[]{:S(2)}, u32[]{:S(2)}) collective-permute-start(bf16[8,256,128]{2,1,0:T(8,128)(2,1)S(1)} %shard_map.88.refs_4_.refs_2_), channel_id=1, source_target_pairs={{0,1},{1,0},{2,3},{3,2},{4,5},{5,4},{6,7},{7,6},{8,9},{9,8},{10,11... | collective-permute-start | bytes 1572872 | tf_op jit(solution)/shard_map/ppermute | solution.py:339
  34.3 11.0 %collective-permute-start.7 = (bf16[8,256,128]{2,1,0:T(8,128)(2,1)S(1)}, bf16[8,256,128]{2,1,0:T(8,128)(2,1)S(1)}, u32[]{:S(2)}, u32[]{:S(2)}) collective-permute-start(bf16[8,256,128]{2,1,0:T(8,128)(2,1)S(1)} %shard_map.88.refs_4_.refs_2_), channel_id=1, source_target_pairs={{4,0},{8,4},{12,8},{14,12},{10,14},{6,10},{2,6},{0,2},{1,5},{5,9},... | collective-permute-start | bytes 1572872 | tf_op jit(solution)/shard_map/ppermute | solution.py:336
  38.1 9.5 %collective-permute-start.13 = (bf16[8,256,128]{2,1,0:T(8,128)(2,1)S(1)}, bf16[8,256,128]{2,1,0:T(8,128)(2,1)S(1)}, u32[]{:S(2)}, u32[]{:S(2)}) collective-permute-start(bf16[8,256,128]{2,1,0:T(8,128)(2,1)S(1)} %shard_map.90.refs_4_.refs_2_), channel_id=1, source_target_pairs={{0,1},{1,0},{2,3},{3,2},{4,5},{5,4},{6,7},{7,6},{8,9},{9,8},{10,11... | collective-permute-start | bytes 1572872 | tf_op jit(solution)/shard_map/ppermute | solution.py:339
  39.0 11.0 %collective-permute-start.12 = (bf16[8,256,128]{2,1,0:T(8,128)(2,1)S(1)}, bf16[8,256,128]{2,1,0:T(8,128)(2,1)S(1)}, u32[]{:S(2)}, u32[]{:S(2)}) collective-permute-start(bf16[8,256,128]{2,1,0:T(8,128)(2,1)S(1)} %shard_map.90.refs_4_.refs_2_), channel_id=1, source_target_pairs={{0,4},{4,8},{8,12},{12,14},{14,10},{10,6},{6,2},{2,0},{5,1},{9,5},... | collective-permute-start | bytes 1572872 | tf_op jit(solution)/shard_map/ppermute | solution.py:336
  45.3 11.3 %collective-permute-start.14 = (bf16[8,256,128]{2,1,0:T(8,128)(2,1)S(1)}, bf16[8,256,128]{2,1,0:T(8,128)(2,1)S(1)}, u32[]{:S(2)}, u32[]{:S(2)}) collective-permute-start(bf16[8,256,128]{2,1,0:T(8,128)(2,1)S(1)} %shard_map.92.refs_4_.refs_2_), channel_id=1, source_target_pairs={{4,0},{8,4},{12,8},{14,12},{10,14},{6,10},{2,6},{0,2},{1,5},{5,9},... | collective-permute-start | bytes 1572872 | tf_op jit(solution)/shard_map/ppermute | solution.py:336
  50.0 8.5 %collective-permute-start.18 = (bf16[8,256,128]{2,1,0:T(8,128)(2,1)S(1)}, bf16[8,256,128]{2,1,0:T(8,128)(2,1)S(1)}, u32[]{:S(2)}, u32[]{:S(2)}) collective-permute-start(bf16[8,256,128]{2,1,0:T(8,128)(2,1)S(1)} %shard_map.94.refs_4_.refs_2_), channel_id=1, source_target_pairs={{0,1},{1,0},{2,3},{3,2},{4,5},{5,4},{6,7},{7,6},{8,9},{9,8},{10,11... | collective-permute-start | bytes 1572872 | tf_op jit(solution)/shard_map/ppermute | solution.py:339
  50.1 10.7 %collective-permute-start.17 = (bf16[8,256,128]{2,1,0:T(8,128)(2,1)S(1)}, bf16[8,256,128]{2,1,0:T(8,128)(2,1)S(1)}, u32[]{:S(2)}, u32[]{:S(2)}) collective-permute-start(bf16[8,256,128]{2,1,0:T(8,128)(2,1)S(1)} %shard_map.94.refs_4_.refs_2_), channel_id=1, source_target_pairs={{0,4},{4,8},{8,12},{12,14},{14,10},{10,6},{6,2},{2,0},{5,1},{9,5},... | collective-permute-start | bytes 1572872 | tf_op jit(solution)/shard_map/ppermute | solution.py:336
  56.6 7.0 %collective-permute-start.16 = (bf16[8,256,128]{2,1,0:T(8,128)(2,1)S(1)}, bf16[8,256,128]{2,1,0:T(8,128)(2,1)S(1)}, u32[]{:S(2)}, u32[]{:S(2)}) collective-permute-start(bf16[8,256,128]{2,1,0:T(8,128)(2,1)S(1)} %shard_map.97.refs_4_.refs_2_), channel_id=1, source_target_pairs={{0,1},{1,0},{2,3},{3,2},{4,5},{5,4},{6,7},{7,6},{8,9},{9,8},{10,11... | collective-permute-start | bytes 1572872 | tf_op jit(solution)/shard_map/ppermute | solution.py:339
  56.6 11.0 %collective-permute-start.15 = (bf16[8,256,128]{2,1,0:T(8,128)(2,1)S(1)}, bf16[8,256,128]{2,1,0:T(8,128)(2,1)S(1)}, u32[]{:S(2)}, u32[]{:S(2)}) collective-permute-start(bf16[8,256,128]{2,1,0:T(8,128)(2,1)S(1)} %shard_map.97.refs_4_.refs_2_), channel_id=1, source_target_pairs={{4,0},{8,4},{12,8},{14,12},{10,14},{6,10},{2,6},{0,2},{1,5},{5,9},... | collective-permute-start | bytes 1572872 | tf_op jit(solution)/shard_map/ppermute | solution.py:336
  60.8 9.3 %collective-permute-start.22 = (bf16[8,256,128]{2,1,0:T(8,128)(2,1)S(1)}, bf16[8,256,128]{2,1,0:T(8,128)(2,1)S(1)}, u32[]{:S(2)}, u32[]{:S(2)}) collective-permute-start(bf16[8,256,128]{2,1,0:T(8,128)(2,1)S(1)} %shard_map.99.refs_4_.refs_2_), channel_id=1, source_target_pairs={{0,1},{1,0},{2,3},{3,2},{4,5},{5,4},{6,7},{7,6},{8,9},{9,8},{10,11... | collective-permute-start | bytes 1572872 | tf_op jit(solution)/shard_map/ppermute | solution.py:339
  62.0 11.1 %collective-permute-start.21 = (bf16[8,256,128]{2,1,0:T(8,128)(2,1)S(1)}, bf16[8,256,128]{2,1,0:T(8,128)(2,1)S(1)}, u32[]{:S(2)}, u32[]{:S(2)}) collective-permute-start(bf16[8,256,128]{2,1,0:T(8,128)(2,1)S(1)} %shard_map.99.refs_4_.refs_2_), channel_id=1, source_target_pairs={{0,4},{4,8},{8,12},{12,14},{14,10},{10,6},{6,2},{2,0},{5,1},{9,5},... | collective-permute-start | bytes 1572872 | tf_op jit(solution)/shard_map/ppermute | solution.py:336
  67.6 7.5 %collective-permute-start.20 = (bf16[8,256,128]{2,1,0:T(8,128)(2,1)S(1)}, bf16[8,256,128]{2,1,0:T(8,128)(2,1)S(1)}, u32[]{:S(2)}, u32[]{:S(2)}) collective-permute-start(bf16[8,256,128]{2,1,0:T(8,128)(2,1)S(1)} %shard_map.101.refs_4_.refs_2_), channel_id=1, source_target_pairs={{0,1},{1,0},{2,3},{3,2},{4,5},{5,4},{6,7},{7,6},{8,9},{9,8},{10,11... | collective-permute-start | bytes 1572872 | tf_op jit(solution)/shard_map/ppermute | solution.py:339
  67.6 10.8 %collective-permute-start.19 = (bf16[8,256,128]{2,1,0:T(8,128)(2,1)S(1)}, bf16[8,256,128]{2,1,0:T(8,128)(2,1)S(1)}, u32[]{:S(2)}, u32[]{:S(2)}) collective-permute-start(bf16[8,256,128]{2,1,0:T(8,128)(2,1)S(1)} %shard_map.101.refs_4_.refs_2_), channel_id=1, source_target_pairs={{4,0},{8,4},{12,8},{14,12},{10,14},{6,10},{2,6},{0,2},{1,5},{5,9},... | collective-permute-start | bytes 1572872 | tf_op jit(solution)/shard_map/ppermute | solution.py:336
  73.2 8.1 %collective-permute-start.26 = (bf16[8,256,128]{2,1,0:T(8,128)(2,1)S(1)}, bf16[8,256,128]{2,1,0:T(8,128)(2,1)S(1)}, u32[]{:S(2)}, u32[]{:S(2)}) collective-permute-start(bf16[8,256,128]{2,1,0:T(8,128)(2,1)S(1)} %shard_map.103.refs_4_.refs_2_), channel_id=1, source_target_pairs={{0,1},{1,0},{2,3},{3,2},{4,5},{5,4},{6,7},{7,6},{8,9},{9,8},{10,11... | collective-permute-start | bytes 1572872 | tf_op jit(solution)/shard_map/ppermute | solution.py:339
  73.2 11.4 %collective-permute-start.25 = (bf16[8,256,128]{2,1,0:T(8,128)(2,1)S(1)}, bf16[8,256,128]{2,1,0:T(8,128)(2,1)S(1)}, u32[]{:S(2)}, u32[]{:S(2)}) collective-permute-start(bf16[8,256,128]{2,1,0:T(8,128)(2,1)S(1)} %shard_map.103.refs_4_.refs_2_), channel_id=1, source_target_pairs={{0,4},{4,8},{8,12},{12,14},{14,10},{10,6},{6,2},{2,0},{5,1},{9,5},... | collective-permute-start | bytes 1572872 | tf_op jit(solution)/shard_map/ppermute | solution.py:336
  79.4 10.1 %collective-permute-start.23 = (bf16[8,256,128]{2,1,0:T(8,128)(2,1)S(1)}, bf16[8,256,128]{2,1,0:T(8,128)(2,1)S(1)}, u32[]{:S(2)}, u32[]{:S(2)}) collective-permute-start(bf16[8,256,128]{2,1,0:T(8,128)(2,1)S(1)} %shard_map.105.refs_4_.refs_2_), channel_id=1, source_target_pairs={{4,0},{8,4},{12,8},{14,12},{10,14},{6,10},{2,6},{0,2},{1,5},{5,9},... | collective-permute-start | bytes 1572872 | tf_op jit(solution)/shard_map/ppermute | solution.py:336
  (18 other events, 87.6 us)

commit v3 on v2

--- a/solution.py
+++ b/solution.py
@@ -8,9 +8,10 @@
 from jax.sharding import PartitionSpec as P
 
 THERMAL = 0.3
+LANES = 128
 SLOTS = 32
 FIRST_SLOTS = 20
-GROUP = 4
+GROUP = 6
 ENTRY_BITS = 5
 
 VMEM = pl.BlockSpec(memory_space=pltpu.VMEM)
@@ -104,13 +105,11 @@
         load(pos).wait()
 
 
-def split_parts(sums, bits, levels, parts):
+def split_parts(sums, me, levels, parts):
     comps, count, share, lower_count = sums.shape
     pieces = [sums]
     for level in levels:
-        side = jnp.broadcast_to(
-            bits[level][None, None, :1], (comps, pieces[0].shape[1] // 2, share, lower_count)
-        ) > 0
+        side = ((me >> level) & 1) == 1
         same, other = [], []
         for piece in pieces:
             halves = piece.reshape(comps, piece.shape[1] // 2, 2, share, lower_count)
@@ -143,21 +142,21 @@
     return jnp.stack(sums)
 
 
-def small_call(body, out_shape, *operands):
+def small_call(body, out_shape, *operands, scalars=()):
     return pl.pallas_call(
         body,
         out_shape=out_shape,
-        in_specs=[VMEM] * len(operands),
+        in_specs=[SMEM] * len(scalars) + [VMEM] * len(operands),
         out_specs=jax.tree.map(lambda _: VMEM, out_shape),
         compiler_params=pltpu.CompilerParams(vmem_limit_bytes=8 * 2**20),
-    )(*operands)
-
-
-def own_outputs(upper_t, moments, comps, bits, factor, group):
+    )(*scalars, *operands)
+
+
+def own_outputs(upper_t, moments, comps, plan, spot, upper_energy, lower_energy, group):
     upper_count = upper_t.shape[0]
     lower_count = moments.shape[2]
     share = upper_count // group
-    levels = bits.shape[0]
+    levels = group.bit_length() - 1
 
     rounds = [[0]] + [list(range(i, min(i + 2, levels))) for i in range(1, levels, 2)]
     left = group
@@ -168,25 +167,32 @@
             1 << len(rounds[number])
         )
 
-    def first(upper_t, moments, bits, *parts):
-        split_parts(project(upper_t, moments, comps, (group, share)), bits, rounds[0], parts)
-
-    def middle(number, n_sums, *refs):
-        total = refs[0][...]
-        for ref in refs[1:n_sums]:
-            total = total + ref[...]
-        split_parts(total, refs[n_sums], rounds[number], refs[n_sums + 1 :])
-
-    def final(n_sums, *refs):
-        total = refs[0][...]
-        for ref in refs[1:n_sums]:
-            total = total + ref[...]
-        factor, strength, intensity = refs[n_sums:]
-        own = total[:, 0]
+    def first(plan, upper_t, moments, *parts):
+        split_parts(project(upper_t, moments, comps, (group, share)), plan[spot], rounds[0], parts)
+
+    def total(refs):
+        result = refs[0][...]
+        for ref in refs[1:]:
+            result = result + ref[...]
+        return result
+
+    def middle(number, n_sums, plan, *refs):
+        split_parts(total(refs[:n_sums]), plan[spot], rounds[number], refs[n_sums:])
+
+    def final(n_sums, plan, *refs):
+        own = total(refs[:n_sums])[:, 0]
+        upper, lower, strength, intensity = refs[n_sums:]
         strength[...] = jnp.sum(own * own, axis=0)
-        intensity[...] = factor[...] * strength[...]
-
-    parts = small_call(first, shapes(0), upper_t, moments, bits)
+        row = plan[spot] * share + lax.broadcasted_iota(jnp.int32, (share, LANES), 0)
+        lane = lax.broadcasted_iota(jnp.int32, (share, LANES), 1)
+        energy = jnp.zeros((share, LANES), jnp.float32)
+        for start in range(0, upper_count, LANES):
+            energy += jnp.where(row == lane + start, upper[pl.ds(start, LANES)].reshape(1, LANES), 0.0)
+        below = lower[...].reshape(1, lower_count)
+        wavenumber = jnp.sum(energy, axis=1, keepdims=True) - below
+        intensity[...] = wavenumber**3 * jnp.exp(-below / THERMAL) * strength[...]
+
+    parts = small_call(first, shapes(0), upper_t, moments, scalars=(plan,))
     for number, used in enumerate(rounds):
         left >>= len(used)
         terms = [parts[0]]
@@ -195,10 +201,11 @@
             terms.append(lax.ppermute(parts[choice], "blk", [(d, d ^ mask) for d in range(group)]))
         if number + 1 < len(rounds):
             parts = small_call(
-                functools.partial(middle, number + 1, len(terms)), shapes(number + 1), *terms, bits
+                functools.partial(middle, number + 1, len(terms)), shapes(number + 1), *terms, scalars=(plan,)
             )
     out = [jax.ShapeDtypeStruct((share, lower_count), jnp.float32)] * 2
-    return small_call(functools.partial(final, len(terms)), out, *terms, factor)
+    body = functools.partial(final, len(terms))
+    return small_call(body, out, *terms, upper_energy, lower_energy, scalars=(plan,))
 
 
 def run_stage(stage, reach, plan, layout, dipole, pieces, lower_count, state, behind=()):
@@ -273,13 +280,13 @@
     return pl.pallas_call(
         body,
         out_shape=jax.ShapeDtypeStruct((count,) + array.shape[1:], array.dtype),
-        in_specs=[pl.BlockSpec(memory_space=pltpu.HBM)] + [SMEM] * len(needed),
+        in_specs=[ANY] + [SMEM] * len(needed),
         out_specs=ANY,
         compiler_params=pltpu.CompilerParams(vmem_limit_bytes=2**20),
-    )(array, *needed)
-
-
-def sorted_entries(stage, slot, n_stages, low_bits):
+    )(pltpu.with_memory_space_constraint(array, pltpu.HBM), *needed)
+
+
+def sorted_entries(stage, slot, n_stages, low_bits, me):
     rows, count = stage.shape
     total = rows * count
     row = lax.broadcasted_iota(jnp.int32, stage.shape, 0)
@@ -287,20 +294,21 @@
     code = ((((row << ENTRY_BITS) + entry) << (low_bits + 1)) + slot).reshape(total)
     key = (stage * total + row * count + entry).reshape(total)
     rank = jnp.sum((key[None, :] < key[:, None]).astype(jnp.int32), axis=1)
-    length = -(-(total + n_stages + 1) // 128) * 128
+    spot = total + n_stages + 1
+    length = -(-(spot + 1) // LANES) * LANES
     place = jnp.arange(length, dtype=jnp.int32)
     codes = jnp.sum(jnp.where(rank[:, None] == place[None, :], code[:, None], 0), axis=0)
     bounds = jnp.sum((stage.reshape(total, 1) < place[None, :] - total).astype(jnp.int32), axis=0)
-    return pl.pallas_call(
+    return spot, pl.pallas_call(
         lambda source, plan: pltpu.sync_copy(source, plan),
         out_shape=pltpu.SMEM((length,), jnp.int32),
         in_specs=[ANY],
         out_specs=SMEM,
         compiler_params=pltpu.CompilerParams(vmem_limit_bytes=2**20),
-    )(jnp.where(place < total, codes, bounds))
-
-
-def ring_moments(dipole, block_cols, lower_blocks, upper_vecs, group, needed):
+    )(jnp.where(place < total, codes, jnp.where(place == spot, me, bounds)))
+
+
+def ring_moments(dipole, block_cols, lower_blocks, upper_vecs, group):
     rows = dipole.shape[0]
     lower_count = lower_blocks.shape[2]
     me = lax.axis_index("blk")
@@ -326,10 +334,10 @@
     hops = jnp.where(forward, mine - theirs, theirs - mine) % chips
     other_core = (owner + me) % 2
     stage = 1 + jnp.where(hops == 0, other_core, 2 * hops + part)
-    index = jnp.where(hops == 0, local, local % half)
+    other = jnp.where(hops == 0, part, other_core)
     n_stages = 2 * chips + 1
-    layout = (block_cols.size, (rows - 1).bit_length())
-    plan = sorted_entries(stage, (other_core << layout[1]) + index, n_stages, layout[1])
+    layout = (block_cols.size, (half - 1).bit_length())
+    spot, plan = sorted_entries(stage, (other << layout[1]) + local % half, n_stages, layout[1], me)
     reach = [FIRST_SLOTS] + [SLOTS] * (n_stages - 1)
 
     def hop(array, p):
@@ -341,12 +349,14 @@
     def compute(number, arrived, state, *behind):
         return run_stage(number, reach, plan, layout, dipole, arrived, lower_count, state, behind)
 
-    flying = [hop(part_of(lower_blocks, 0, half), 0)]
-    there = cross(lower_blocks)
+    first = part_of(lower_blocks, 0, half)
+    flying = [hop(first, 0)]
+    there = [cross(first)]
     second = part_of(lower_blocks, half, half, plan)
     flying.append(hop(second, 1))
-    waiting = [(1, [lower_blocks]), (2, [there])]
-    state, done = compute(0, [], None, second, *needed)
+    there.append(cross(second))
+    waiting = [(1, [first, second]), (2, there)]
+    state, done = compute(0, [], None, second)
     upper_t = None
     for h in range(1, chips):
         for p in range(2):
@@ -360,13 +370,13 @@
                 done = upper_t = transposed(upper_vecs, done)
     for number, arrived in waiting:
         state, done = compute(number, arrived, state)
-    return state[0], upper_t
+    return state[0], upper_t, spot, plan
 
 
 def gathered_moments(dipole, block_cols, lower_blocks):
     gathered = lax.all_gather(lower_blocks, "blk", axis=0, tiled=True)
     layout = (block_cols.size, (gathered.shape[0] - 1).bit_length())
-    plan = sorted_entries(jnp.zeros_like(block_cols), block_cols, 1, layout[1])
+    _, plan = sorted_entries(jnp.zeros_like(block_cols), block_cols, 1, layout[1], 0)
     state, _ = run_stage(0, [SLOTS], plan, layout, dipole, [gathered], lower_blocks.shape[2], None)
     return state[0]
 
@@ -393,17 +403,13 @@
     me = lax.axis_index("blk")
     lower_blocks = lower_vecs.reshape(rows, block, lower_vecs.shape[1])
     share = upper_vecs.shape[1] // group
+    comps = dipole.shape[2]
+    if rows % 2 == 0 and share % 8 == 0 and upper_vecs.shape[1] % LANES == 0 and group >= 8 and group & (group - 1) == 0:
+        moments, upper_t, spot, plan = ring_moments(dipole, block_cols, lower_blocks, upper_vecs, group)
+        return own_outputs(upper_t, moments, comps, plan, spot, upper_energy, lower_energy, group)
     energy = lax.dynamic_slice_in_dim(upper_energy, me * share, share, 0)
     wavenumber = energy[:, None] - lower_energy[None, :]
     factor = wavenumber**3 * jnp.exp(-lower_energy / THERMAL)[None, :]
-    comps = dipole.shape[2]
-    if rows % 2 == 0 and share % 8 == 0 and group >= 8 and group & (group - 1) == 0:
-        levels = jnp.arange(group.bit_length() - 1, dtype=jnp.int32)
-        bits = jnp.broadcast_to(((me >> levels) & 1)[:, None, None], (levels.shape[0], 8, 128))
-        moments, upper_t = ring_moments(
-            dipole, block_cols, lower_blocks, upper_vecs, group, [factor, bits]
-        )
-        return own_outputs(upper_t, moments, comps, bits, factor, group)
     moments = gathered_moments(dipole, block_cols, lower_blocks)
     upper_t = upper_vecs.T
 

time: 114 us -> 113 us (level)
  local copies, waits for them, and re-layouts: 3.82 us -> 0.55 us
  Pallas kernels: 49.8 us -> 52.5 us
  waiting for transfers between devices: 18.3 us -> 20.2 us
  starting transfers between devices: 37.3 us -> 35.9 us
  other arithmetic: 3.3 us -> 1.91 us
    ppermute x14, starting transfers between devices: 25 us -> 21.5 us  [hop(): return lax.ppermute(array, 'blk', ways[p])]
    ppermute x14, waiting for transfers between devices: 9.06 us -> 12.5 us  [hop(): return lax.ppermute(array, 'blk', ways[p])]
    ppermute x5, starting transfers between devices: 7.17 us -> 10.2 us  [own_outputs(): lax.ppermute(parts[choice], 'blk', [(d, d ^ mask) for d in range(group)])]
    unnamed x16 -> x6, local copies, waits for them, and re-layouts: 2.74 us -> 0.28 us
    pallas_call x2, Pallas kernels: 0.07 us -> 2.09 us  [part_of(): pl.pallas_call(body, out_shape=jax.ShapeDtypeStruct((count,) + array.shap...]
    ppermute x5, waiting for transfers between devices: 9.21 us -> 7.73 us  [own_outputs(): lax.ppermute(parts[choice], 'blk', [(d, d ^ mask) for d in range(group)])]
    ppermute x15 -> x16, starting transfers between devices: 5.1 us -> 4.21 us  [cross(): return lax.ppermute(array, 'blk', sibling)]
  transfers between devices with their start and end apart: 34 -> 35, of which waited for: 12 -> 12; matrix products, arithmetic and copies ran while one was open for 4% -> 2% of each run, Pallas kernels for 39% -> 42%
where the time goes in v3:
time: 113 us; the launch traced here: 112 us
  Pallas kernels  52.5 us (46%)
  starting transfers between devices  35.9 us (32%)
  waiting for transfers between devices  20.2 us (18%)
  other arithmetic  1.91 us (2%)
    pallas_call x17, Pallas kernels, run_stage(): pl.pallas_call(functools.partial(stage_body, stage, first, reach, layout,...  46.7 us
    ppermute x14, starting transfers between devices, hop(): return lax.ppermute(array, 'blk', ways[p])  21.5 us
    ppermute x14, waiting for transfers between devices, hop(): return lax.ppermute(array, 'blk', ways[p])  12.5 us
    ppermute x5, starting transfers between devices, own_outputs(): lax.ppermute(parts[choice], 'blk', [(d, d ^ mask) for d in range(group)])  10.2 us
    ppermute x5, waiting for transfers between devices, own_outputs(): lax.ppermute(parts[choice], 'blk', [(d, d ^ mask) for d in range(group)])  7.73 us
    ppermute x16, starting transfers between devices, cross(): return lax.ppermute(array, 'blk', sibling)  4.21 us
    pallas_call x4, Pallas kernels, small_call(): pl.pallas_call(body, out_shape=out_shape, in_specs=[SMEM] * len(scalars)...  2.52 us
  transfers between devices with their start and end apart: 35, of which 12 were waited for; matrix products, arithmetic and copies ran while one was open for 2% of the time, Pallas kernels for 42%

profile of v3, /device:TPU:0, one launch (start us, length us, event | category | flops | bytes accessed | tf_op | source)
XLA Modules:
  0.0 112.2 jit_solution(2964845414925735684)
XLA Ops:
  1.7 3.0 %collective-permute-start.3 = (bf16[8,256,128]{2,1,0:T(8,128)(2,1)S(1)}, bf16[8,256,128]{2,1,0:T(8,128)(2,1)S(1)}, u32[]{:S(2)}, u32[]{:S(2)}) collective-permute-start(bf16[8,256,128]{2,1,0:T(8,128)(2,1)S(1)} %shard_map.79.refs_2_), channel_id=1, source_target_pairs={{0,4},{4,8},{8,12},{12,14},{14,10},{10,6},{6,2},{2,0},{5,1},{9,5},... | collective-permute-start | bytes 1572872 | tf_op jit(solution)/shard_map/ppermute | solution.py:344
  9.6 3.5 %shard_map.80 = (f32[16,768,128]{2,1,0:T(8,128)S(1)}, bf16[32,3,256,256]{3,2,1,0:T(8,128)(2,1)S(1)}, f32[8,128]{1,0:T(8,128)S(1)}) custom-call(s32[256]{0:T(256)S(4)} %shard_map.77.refs_1_.refs_0_.plan, bf16[16,12,3,256,256]{4,3,2,1,0:T(8,128)(2,1)} %refs_1_.33, bf16[8,256,128]{2,1,0:T(8,128)(2,1)S(1)} %shard_map.78.refs_2_.refs_3_), custom_call_target="tpu_custom_call" | custom-call | flops 603979776 | bytes 4718592 | tf_op jit(solution)/shard_map/pallas_call | solution.py:224
  15.5 2.9 %shard_map.82 = (f32[16,768,128]{2,1,0:T(8,128)S(1)}, bf16[32,3,256,256]{3,2,1,0:T(8,128)(2,1)S(1)}, f32[8,128]{1,0:T(8,128)}) custom-call(s32[256]{0:T(256)S(4)} %shard_map.77.refs_1_.refs_0_.plan, bf16[16,12,3,256,256]{4,3,2,1,0:T(8,128)(2,1)} %refs_1_.33, ...), custom_call_target="tpu_custom_call", output_to_operand_aliasing={{0}: (5, {}), {1}: (6, {})} | custom-call | flops 603979776 | bytes 4718592 | tf_op jit(solution)/shard_map/pallas_call | solution.py:224
  18.5 3.1 %shard_map.83 = (f32[16,768,128]{2,1,0:T(8,128)S(1)}, bf16[32,3,256,256]{3,2,1,0:T(8,128)(2,1)S(1)}, f32[8,128]{1,0:T(8,128)S(1)}) custom-call(s32[256]{0:T(256)S(4)} %shard_map.77.refs_1_.refs_0_.plan, bf16[16,12,3,256,256]{4,3,2,1,0:T(8,128)(2,1)} %refs_1_.33, ...), custom_call_target="tpu_custom_call", output_to_operand_aliasing={{0}: (5, {}), {1}: (6, {})} | custom-call | flops 603979776 | bytes 4718592 | tf_op jit(solution)/shard_map/pallas_call | solution.py:224
  22.9 2.6 %shard_map.85 = (f32[16,768,128]{2,1,0:T(8,128)S(1)}, bf16[32,3,256,256]{3,2,1,0:T(8,128)(2,1)S(1)}, f32[8,128]{1,0:T(8,128)S(1)}) custom-call(s32[256]{0:T(256)S(4)} %shard_map.77.refs_1_.refs_0_.plan, bf16[16,12,3,256,256]{4,3,2,1,0:T(8,128)(2,1)} %refs_1_.33, ...), custom_call_target="tpu_custom_call", output_to_operand_aliasing={{0}: (5, {}), {1}: (6, {})} | custom-call | flops 603979776 | bytes 4718592 | tf_op jit(solution)/shard_map/pallas_call | solution.py:224
  27.4 3.0 %shard_map.87 = (f32[16,768,128]{2,1,0:T(8,128)S(1)}, bf16[32,3,256,256]{3,2,1,0:T(8,128)(2,1)S(1)}, f32[8,128]{1,0:T(8,128)S(1)}) custom-call(s32[256]{0:T(256)S(4)} %shard_map.77.refs_1_.refs_0_.plan, bf16[16,12,3,256,256]{4,3,2,1,0:T(8,128)(2,1)} %refs_1_.33, ...), custom_call_target="tpu_custom_call", output_to_operand_aliasing={{0}: (5, {}), {1}: (6, {})} | custom-call | flops 603979776 | bytes 4718592 | tf_op jit(solution)/shard_map/pallas_call | solution.py:224
  30.4 2.6 %collective-permute-done.4.refs_0_ = bf16[8,256,128]{2,1,0:T(8,128)(2,1)S(1)} collective-permute-done((bf16[8,256,128]{2,1,0:T(8,128)(2,1)S(1)}, bf16[8,256,128]{2,1,0:T(8,128)(2,1)S(1)}, u32[]{:S(2)}, u32[]{:S(2)}) %collective-permute-start.4) | collective-permute-done | bytes 524320 | tf_op jit(solution)/shard_map/ppermute | solution.py:344
  33.8 3.0 %shard_map.89 = (f32[16,768,128]{2,1,0:T(8,128)S(1)}, bf16[32,3,256,256]{3,2,1,0:T(8,128)(2,1)S(1)}, f32[8,128]{1,0:T(8,128)S(1)}) custom-call(s32[256]{0:T(256)S(4)} %shard_map.77.refs_1_.refs_0_.plan, bf16[16,12,3,256,256]{4,3,2,1,0:T(8,128)(2,1)} %refs_1_.33, ...), custom_call_target="tpu_custom_call", output_to_operand_aliasing={{0}: (5, {}), {1}: (6, {})} | custom-call | flops 603979776 | bytes 4718592 | tf_op jit(solution)/shard_map/pallas_call | solution.py:224
  38.5 2.7 %shard_map.91 = (f32[16,768,128]{2,1,0:T(8,128)S(1)}, bf16[32,3,256,256]{3,2,1,0:T(8,128)(2,1)S(1)}, f32[8,128]{1,0:T(8,128)S(1)}) custom-call(s32[256]{0:T(256)S(4)} %shard_map.77.refs_1_.refs_0_.plan, bf16[16,12,3,256,256]{4,3,2,1,0:T(8,128)(2,1)} %refs_1_.33, ...), custom_call_target="tpu_custom_call", output_to_operand_aliasing={{0}: (5, {}), {1}: (6, {})} | custom-call | flops 603979776 | bytes 4718592 | tf_op jit(solution)/shard_map/pallas_call | solution.py:224
  41.2 3.0 %collective-permute-done.8.refs_0_ = bf16[8,256,128]{2,1,0:T(8,128)(2,1)S(1)} collective-permute-done((bf16[8,256,128]{2,1,0:T(8,128)(2,1)S(1)}, bf16[8,256,128]{2,1,0:T(8,128)(2,1)S(1)}, u32[]{:S(2)}, u32[]{:S(2)}) %collective-permute-start.8) | collective-permute-done | bytes 524320 | tf_op jit(solution)/shard_map/ppermute | solution.py:344
  47.6 2.5 %collective-permute-start.18 = (bf16[8,256,128]{2,1,0:T(8,128)(2,1)S(1)}, bf16[8,256,128]{2,1,0:T(8,128)(2,1)S(1)}, u32[]{:S(2)}, u32[]{:S(2)}) collective-permute-start(bf16[8,256,128]{2,1,0:T(8,128)(2,1)S(1)} %shard_map.94.refs_4_.refs_2_), channel_id=1, source_target_pairs={{0,4},{4,8},{8,12},{12,14},{14,10},{10,6},{6,2},{2,0},{5,1},{9,5},... | collective-permute-start | bytes 1572872 | tf_op jit(solution)/shard_map/ppermute | solution.py:344
  50.1 2.3 %shard_map.95 = (f32[16,768,128]{2,1,0:T(8,128)S(1)}, bf16[32,3,256,256]{3,2,1,0:T(8,128)(2,1)S(1)}, f32[8,128]{1,0:T(8,128)S(1)}) custom-call(s32[256]{0:T(256)S(4)} %shard_map.77.refs_1_.refs_0_.plan, bf16[16,12,3,256,256]{4,3,2,1,0:T(8,128)(2,1)} %refs_1_.33, ...), custom_call_target="tpu_custom_call", output_to_operand_aliasing={{0}: (5, {}), {1}: (6, {})} | custom-call | flops 603979776 | bytes 4718592 | tf_op jit(solution)/shard_map/pallas_call | solution.py:224
  53.3 2.6 %collective-permute-done.15.refs_0_ = bf16[8,256,128]{2,1,0:T(8,128)(2,1)S(1)} collective-permute-done((bf16[8,256,128]{2,1,0:T(8,128)(2,1)S(1)}, bf16[8,256,128]{2,1,0:T(8,128)(2,1)S(1)}, u32[]{:S(2)}, u32[]{:S(2)}) %collective-permute-start.15) | collective-permute-done | bytes 524320 | tf_op jit(solution)/shard_map/ppermute | solution.py:344
  57.1 2.3 %shard_map.98 = (f32[16,768,128]{2,1,0:T(8,128)S(1)}, bf16[32,3,256,256]{3,2,1,0:T(8,128)(2,1)S(1)}, f32[8,128]{1,0:T(8,128)S(1)}) custom-call(s32[256]{0:T(256)S(4)} %shard_map.77.refs_1_.refs_0_.plan, bf16[16,12,3,256,256]{4,3,2,1,0:T(8,128)(2,1)} %refs_1_.33, ...), custom_call_target="tpu_custom_call", output_to_operand_aliasing={{0}: (5, {}), {1}: (6, {})} | custom-call | flops 603979776 | bytes 4718592 | tf_op jit(solution)/shard_map/pallas_call | solution.py:224
  61.3 2.9 %shard_map.100 = (f32[16,768,128]{2,1,0:T(8,128)S(1)}, bf16[32,3,256,256]{3,2,1,0:T(8,128)(2,1)S(1)}, f32[8,128]{1,0:T(8,128)S(1)}) custom-call(s32[256]{0:T(256)S(4)} %shard_map.77.refs_1_.refs_0_.plan, bf16[16,12,3,256,256]{4,3,2,1,0:T(8,128)(2,1)} %refs_1_.33, ...), custom_call_target="tpu_custom_call", output_to_operand_aliasing={{0}: (5, {}), {1}: (6, {})} | custom-call | flops 603979776 | bytes 4718592 | tf_op jit(solution)/shard_map/pallas_call | solution.py:224
  64.2 2.8 %collective-permute-done.16.refs_0_ = bf16[8,256,128]{2,1,0:T(8,128)(2,1)S(1)} collective-permute-done((bf16[8,256,128]{2,1,0:T(8,128)(2,1)S(1)}, bf16[8,256,128]{2,1,0:T(8,128)(2,1)S(1)}, u32[]{:S(2)}, u32[]{:S(2)}) %collective-permute-start.16) | collective-permute-done | bytes 524320 | tf_op jit(solution)/shard_map/ppermute | solution.py:344
  68.4 3.1 %shard_map.102 = (f32[16,768,128]{2,1,0:T(8,128)S(1)}, bf16[32,3,256,256]{3,2,1,0:T(8,128)(2,1)S(1)}, f32[8,128]{1,0:T(8,128)S(1)}) custom-call(s32[256]{0:T(256)S(4)} %shard_map.77.refs_1_.refs_0_.plan, bf16[16,12,3,256,256]{4,3,2,1,0:T(8,128)(2,1)} %refs_1_.33, ...), custom_call_target="tpu_custom_call", output_to_operand_aliasing={{0}: (5, {}), {1}: (6, {})} | custom-call | flops 603979776 | bytes 4718592 | tf_op jit(solution)/shard_map/pallas_call | solution.py:224
  71.6 2.6 %collective-permute-start.26 = (bf16[8,256,128]{2,1,0:T(8,128)(2,1)S(1)}, bf16[8,256,128]{2,1,0:T(8,128)(2,1)S(1)}, u32[]{:S(2)}, u32[]{:S(2)}) collective-permute-start(bf16[8,256,128]{2,1,0:T(8,128)(2,1)S(1)} %shard_map.103.refs_4_.refs_2_), channel_id=1, source_target_pairs={{0,4},{4,8},{8,12},{12,14},{14,10},{10,6},{6,2},{2,0},{5,1},{9,5},... | collective-permute-start | bytes 1572872 | tf_op jit(solution)/shard_map/ppermute | solution.py:344
  74.2 3.0 %shard_map.104 = (f32[16,768,128]{2,1,0:T(8,128)S(1)}, bf16[32,3,256,256]{3,2,1,0:T(8,128)(2,1)S(1)}, f32[8,128]{1,0:T(8,128)S(1)}) custom-call(s32[256]{0:T(256)S(4)} %shard_map.77.refs_1_.refs_0_.plan, bf16[16,12,3,256,256]{4,3,2,1,0:T(8,128)(2,1)} %refs_1_.33, ...), custom_call_target="tpu_custom_call", output_to_operand_aliasing={{0}: (5, {}), {1}: (6, {})} | custom-call | flops 603979776 | bytes 4718592 | tf_op jit(solution)/shard_map/pallas_call | solution.py:224
  77.7 3.0 %collective-permute-start.24 = (bf16[8,256,128]{2,1,0:T(8,128)(2,1)S(1)}, bf16[8,256,128]{2,1,0:T(8,128)(2,1)S(1)}, u32[]{:S(2)}, u32[]{:S(2)}) collective-permute-start(bf16[8,256,128]{2,1,0:T(8,128)(2,1)S(1)} %shard_map.105.refs_4_.refs_2_), channel_id=1, source_target_pairs={{4,0},{8,4},{12,8},{14,12},{10,14},{6,10},{2,6},{0,2},{1,5},{5,9},... | collective-permute-start | bytes 1572872 | tf_op jit(solution)/shard_map/ppermute | solution.py:344
  80.7 3.1 %shard_map.106 = (f32[16,768,128]{2,1,0:T(8,128)S(1)}, bf16[32,3,256,256]{3,2,1,0:T(8,128)(2,1)S(1)}, f32[8,128]{1,0:T(8,128)S(1)}) custom-call(s32[256]{0:T(256)S(4)} %shard_map.77.refs_1_.refs_0_.plan, bf16[16,12,3,256,256]{4,3,2,1,0:T(8,128)(2,1)} %refs_1_.33, ...), custom_call_target="tpu_custom_call", output_to_operand_aliasing={{0}: (5, {}), {1}: (6, {})} | custom-call | flops 603979776 | bytes 4718592 | tf_op jit(solution)/shard_map/pallas_call | solution.py:224
  83.8 3.1 %shard_map.108 = (f32[16,768,128]{2,1,0:T(8,128)S(1)}, bf16[32,3,256,256]{3,2,1,0:T(8,128)(2,1)S(1)}, f32[8,128]{1,0:T(8,128)S(1)}) custom-call(s32[256]{0:T(256)S(4)} %shard_map.77.refs_1_.refs_0_.plan, bf16[16,12,3,256,256]{4,3,2,1,0:T(8,128)(2,1)} %refs_1_.33, ...), custom_call_target="tpu_custom_call", output_to_operand_aliasing={{0}: (5, {}), {1}: (6, {})} | custom-call | flops 603979776 | bytes 4718592 | tf_op jit(solution)/shard_map/pallas_call | solution.py:224
  96.0 4.3 %collective-permute-start.31 = (f32[3,2,16,128]{3,2,1,0:T(8,128)S(1)}, f32[3,2,16,128]{3,2,1,0:T(8,128)S(1)}, u32[]{:S(2)}, u32[]{:S(2)}) collective-permute-start(f32[3,2,16,128]{3,2,1,0:T(8,128)S(1)} %get-tuple-element.107), channel_id=1, source_target_pairs={{0,2},{1,3},{2,0},{3,1},{4,6},{5,7},{6,4},{7,5},{8,10},{9,11},{10,... | collective-permute-start | bytes 147464 | tf_op jit(solution)/shard_map/ppermute | solution.py:201
  106.6 3.0 %collective-permute-start.34 = (f32[3,1,16,128]{3,2,1,0:T(8,128)S(1)}, f32[3,1,16,128]{3,2,1,0:T(8,128)S(1)}, u32[]{:S(2)}, u32[]{:S(2)}) collective-permute-start(f32[3,1,16,128]{3,2,1,0:T(8,128)S(1)} %get-tuple-element.111), channel_id=1, source_target_pairs={{0,8},{1,9},{2,10},{3,11},{4,12},{5,13},{6,14},{7,15},{8,0},{9,1},... | collective-permute-start | bytes 73736 | tf_op jit(solution)/shard_map/ppermute | solution.py:201
  (102 shorter events, 41.2 us)
Async XLA Ops:
  1.7 11.4 %collective-permute-start.3 = (bf16[8,256,128]{2,1,0:T(8,128)(2,1)S(1)}, bf16[8,256,128]{2,1,0:T(8,128)(2,1)S(1)}, u32[]{:S(2)}, u32[]{:S(2)}) collective-permute-start(bf16[8,256,128]{2,1,0:T(8,128)(2,1)S(1)} %shard_map.79.refs_2_), channel_id=1, source_target_pairs={{0,4},{4,8},{8,12},{12,14},{14,10},{10,6},{6,2},{2,0},{5,1},{9,5},... | collective-permute-start | bytes 1572872 | tf_op jit(solution)/shard_map/ppermute | solution.py:344
  8.5 9.9 %collective-permute-start.2 = (bf16[8,256,128]{2,1,0:T(8,128)(2,1)S(1)}, bf16[8,256,128]{2,1,0:T(8,128)(2,1)S(1)}, u32[]{:S(2)}, u32[]{:S(2)}) collective-permute-start(bf16[8,256,128]{2,1,0:T(8,128)(2,1)S(1)} %shard_map.78.refs_2_.refs_3_), channel_id=1, source_target_pairs={{0,1},{1,0},{2,3},{3,2},{4,5},{5,4},{6,7},{7,6},{8,9},{9,8},{10,11... | collective-permute-start | bytes 1572872 | tf_op jit(solution)/shard_map/ppermute | solution.py:347
  8.5 9.9 %collective-permute-start.1 = (bf16[8,256,128]{2,1,0:T(8,128)(2,1)S(1)}, bf16[8,256,128]{2,1,0:T(8,128)(2,1)S(1)}, u32[]{:S(2)}, u32[]{:S(2)}) collective-permute-start(bf16[8,256,128]{2,1,0:T(8,128)(2,1)S(1)} %shard_map.79.refs_2_), channel_id=1, source_target_pairs={{0,1},{1,0},{2,3},{3,2},{4,5},{5,4},{6,7},{7,6},{8,9},{9,8},{10,11... | collective-permute-start | bytes 1572872 | tf_op jit(solution)/shard_map/ppermute | solution.py:347
  9.0 12.6 %collective-permute-start = (bf16[8,256,128]{2,1,0:T(8,128)(2,1)S(1)}, bf16[8,256,128]{2,1,0:T(8,128)(2,1)S(1)}, u32[]{:S(2)}, u32[]{:S(2)}) collective-permute-start(bf16[8,256,128]{2,1,0:T(8,128)(2,1)S(1)} %shard_map.78.refs_2_.refs_3_), channel_id=1, source_target_pairs={{4,0},{8,4},{12,8},{14,12},{10,14},{6,10},{2,6},{0,2},{1,5},{5,9},... | collective-permute-start | bytes 1572872 | tf_op jit(solution)/shard_map/ppermute | solution.py:344
  13.1 9.8 %collective-permute-start.7 = (bf16[8,256,128]{2,1,0:T(8,128)(2,1)S(1)}, bf16[8,256,128]{2,1,0:T(8,128)(2,1)S(1)}, u32[]{:S(2)}, u32[]{:S(2)}) collective-permute-start(bf16[8,256,128]{2,1,0:T(8,128)(2,1)S(1)} %shard_map.81.refs_4_.refs_2_), channel_id=1, source_target_pairs={{0,1},{1,0},{2,3},{3,2},{4,5},{5,4},{6,7},{7,6},{8,9},{9,8},{10,11... | collective-permute-start | bytes 1572872 | tf_op jit(solution)/shard_map/ppermute | solution.py:347
  13.9 11.6 %collective-permute-start.6 = (bf16[8,256,128]{2,1,0:T(8,128)(2,1)S(1)}, bf16[8,256,128]{2,1,0:T(8,128)(2,1)S(1)}, u32[]{:S(2)}, u32[]{:S(2)}) collective-permute-start(bf16[8,256,128]{2,1,0:T(8,128)(2,1)S(1)} %shard_map.81.refs_4_.refs_2_), channel_id=1, source_target_pairs={{0,4},{4,8},{8,12},{12,14},{14,10},{10,6},{6,2},{2,0},{5,1},{9,5},... | collective-permute-start | bytes 1572872 | tf_op jit(solution)/shard_map/ppermute | solution.py:344
  21.7 11.3 %collective-permute-start.4 = (bf16[8,256,128]{2,1,0:T(8,128)(2,1)S(1)}, bf16[8,256,128]{2,1,0:T(8,128)(2,1)S(1)}, u32[]{:S(2)}, u32[]{:S(2)}) collective-permute-start(bf16[8,256,128]{2,1,0:T(8,128)(2,1)S(1)} %shard_map.84.refs_4_.refs_2_), channel_id=1, source_target_pairs={{4,0},{8,4},{12,8},{14,12},{10,14},{6,10},{2,6},{0,2},{1,5},{5,9},... | collective-permute-start | bytes 1572872 | tf_op jit(solution)/shard_map/ppermute | solution.py:344
  25.5 8.3 %collective-permute-start.11 = (bf16[8,256,128]{2,1,0:T(8,128)(2,1)S(1)}, bf16[8,256,128]{2,1,0:T(8,128)(2,1)S(1)}, u32[]{:S(2)}, u32[]{:S(2)}) collective-permute-start(bf16[8,256,128]{2,1,0:T(8,128)(2,1)S(1)} %shard_map.86.refs_4_.refs_2_), channel_id=1, source_target_pairs={{0,1},{1,0},{2,3},{3,2},{4,5},{5,4},{6,7},{7,6},{8,9},{9,8},{10,11... | collective-permute-start | bytes 1572872 | tf_op jit(solution)/shard_map/ppermute | solution.py:347
  26.1 10.8 %collective-permute-start.10 = (bf16[8,256,128]{2,1,0:T(8,128)(2,1)S(1)}, bf16[8,256,128]{2,1,0:T(8,128)(2,1)S(1)}, u32[]{:S(2)}, u32[]{:S(2)}) collective-permute-start(bf16[8,256,128]{2,1,0:T(8,128)(2,1)S(1)} %shard_map.86.refs_4_.refs_2_), channel_id=1, source_target_pairs={{0,4},{4,8},{8,12},{12,14},{14,10},{10,6},{6,2},{2,0},{5,1},{9,5},... | collective-permute-start | bytes 1572872 | tf_op jit(solution)/shard_map/ppermute | solution.py:344
  33.0 11.2 %collective-permute-start.8 = (bf16[8,256,128]{2,1,0:T(8,128)(2,1)S(1)}, bf16[8,256,128]{2,1,0:T(8,128)(2,1)S(1)}, u32[]{:S(2)}, u32[]{:S(2)}) collective-permute-start(bf16[8,256,128]{2,1,0:T(8,128)(2,1)S(1)} %shard_map.88.refs_4_.refs_2_), channel_id=1, source_target_pairs={{4,0},{8,4},{12,8},{14,12},{10,14},{6,10},{2,6},{0,2},{1,5},{5,9},... | collective-permute-start | bytes 1572872 | tf_op jit(solution)/shard_map/ppermute | solution.py:344
  36.9 7.6 %collective-permute-start.14 = (bf16[8,256,128]{2,1,0:T(8,128)(2,1)S(1)}, bf16[8,256,128]{2,1,0:T(8,128)(2,1)S(1)}, u32[]{:S(2)}, u32[]{:S(2)}) collective-permute-start(bf16[8,256,128]{2,1,0:T(8,128)(2,1)S(1)} %shard_map.90.refs_4_.refs_2_), channel_id=1, source_target_pairs={{0,1},{1,0},{2,3},{3,2},{4,5},{5,4},{6,7},{7,6},{8,9},{9,8},{10,11... | collective-permute-start | bytes 1572872 | tf_op jit(solution)/shard_map/ppermute | solution.py:347
  37.4 10.0 %collective-permute-start.13 = (bf16[8,256,128]{2,1,0:T(8,128)(2,1)S(1)}, bf16[8,256,128]{2,1,0:T(8,128)(2,1)S(1)}, u32[]{:S(2)}, u32[]{:S(2)}) collective-permute-start(bf16[8,256,128]{2,1,0:T(8,128)(2,1)S(1)} %shard_map.90.refs_4_.refs_2_), channel_id=1, source_target_pairs={{0,4},{4,8},{8,12},{12,14},{14,10},{10,6},{6,2},{2,0},{5,1},{9,5},... | collective-permute-start | bytes 1572872 | tf_op jit(solution)/shard_map/ppermute | solution.py:344
  44.2 11.6 %collective-permute-start.15 = (bf16[8,256,128]{2,1,0:T(8,128)(2,1)S(1)}, bf16[8,256,128]{2,1,0:T(8,128)(2,1)S(1)}, u32[]{:S(2)}, u32[]{:S(2)}) collective-permute-start(bf16[8,256,128]{2,1,0:T(8,128)(2,1)S(1)} %shard_map.92.refs_4_.refs_2_), channel_id=1, source_target_pairs={{4,0},{8,4},{12,8},{14,12},{10,14},{6,10},{2,6},{0,2},{1,5},{5,9},... | collective-permute-start | bytes 1572872 | tf_op jit(solution)/shard_map/ppermute | solution.py:344
  47.3 9.8 %collective-permute-start.19 = (bf16[8,256,128]{2,1,0:T(8,128)(2,1)S(1)}, bf16[8,256,128]{2,1,0:T(8,128)(2,1)S(1)}, u32[]{:S(2)}, u32[]{:S(2)}) collective-permute-start(bf16[8,256,128]{2,1,0:T(8,128)(2,1)S(1)} %shard_map.94.refs_4_.refs_2_), channel_id=1, source_target_pairs={{0,1},{1,0},{2,3},{3,2},{4,5},{5,4},{6,7},{7,6},{8,9},{9,8},{10,11... | collective-permute-start | bytes 1572872 | tf_op jit(solution)/shard_map/ppermute | solution.py:347
  47.6 11.9 %collective-permute-start.18 = (bf16[8,256,128]{2,1,0:T(8,128)(2,1)S(1)}, bf16[8,256,128]{2,1,0:T(8,128)(2,1)S(1)}, u32[]{:S(2)}, u32[]{:S(2)}) collective-permute-start(bf16[8,256,128]{2,1,0:T(8,128)(2,1)S(1)} %shard_map.94.refs_4_.refs_2_), channel_id=1, source_target_pairs={{0,4},{4,8},{8,12},{12,14},{14,10},{10,6},{6,2},{2,0},{5,1},{9,5},... | collective-permute-start | bytes 1572872 | tf_op jit(solution)/shard_map/ppermute | solution.py:344
  55.8 11.2 %collective-permute-start.16 = (bf16[8,256,128]{2,1,0:T(8,128)(2,1)S(1)}, bf16[8,256,128]{2,1,0:T(8,128)(2,1)S(1)}, u32[]{:S(2)}, u32[]{:S(2)}) collective-permute-start(bf16[8,256,128]{2,1,0:T(8,128)(2,1)S(1)} %shard_map.97.refs_4_.refs_2_), channel_id=1, source_target_pairs={{4,0},{8,4},{12,8},{14,12},{10,14},{6,10},{2,6},{0,2},{1,5},{5,9},... | collective-permute-start | bytes 1572872 | tf_op jit(solution)/shard_map/ppermute | solution.py:344
  59.5 8.9 %collective-permute-start.23 = (bf16[8,256,128]{2,1,0:T(8,128)(2,1)S(1)}, bf16[8,256,128]{2,1,0:T(8,128)(2,1)S(1)}, u32[]{:S(2)}, u32[]{:S(2)}) collective-permute-start(bf16[8,256,128]{2,1,0:T(8,128)(2,1)S(1)} %shard_map.99.refs_4_.refs_2_), channel_id=1, source_target_pairs={{0,1},{1,0},{2,3},{3,2},{4,5},{5,4},{6,7},{7,6},{8,9},{9,8},{10,11... | collective-permute-start | bytes 1572872 | tf_op jit(solution)/shard_map/ppermute | solution.py:347
  60.3 11.2 %collective-permute-start.22 = (bf16[8,256,128]{2,1,0:T(8,128)(2,1)S(1)}, bf16[8,256,128]{2,1,0:T(8,128)(2,1)S(1)}, u32[]{:S(2)}, u32[]{:S(2)}) collective-permute-start(bf16[8,256,128]{2,1,0:T(8,128)(2,1)S(1)} %shard_map.99.refs_4_.refs_2_), channel_id=1, source_target_pairs={{0,4},{4,8},{8,12},{12,14},{14,10},{10,6},{6,2},{2,0},{5,1},{9,5},... | collective-permute-start | bytes 1572872 | tf_op jit(solution)/shard_map/ppermute | solution.py:344
  67.0 7.2 %collective-permute-start.21 = (bf16[8,256,128]{2,1,0:T(8,128)(2,1)S(1)}, bf16[8,256,128]{2,1,0:T(8,128)(2,1)S(1)}, u32[]{:S(2)}, u32[]{:S(2)}) collective-permute-start(bf16[8,256,128]{2,1,0:T(8,128)(2,1)S(1)} %shard_map.101.refs_4_.refs_2_), channel_id=1, source_target_pairs={{0,1},{1,0},{2,3},{3,2},{4,5},{5,4},{6,7},{7,6},{8,9},{9,8},{10,11... | collective-permute-start | bytes 1572872 | tf_op jit(solution)/shard_map/ppermute | solution.py:347
  67.0 10.3 %collective-permute-start.20 = (bf16[8,256,128]{2,1,0:T(8,128)(2,1)S(1)}, bf16[8,256,128]{2,1,0:T(8,128)(2,1)S(1)}, u32[]{:S(2)}, u32[]{:S(2)}) collective-permute-start(bf16[8,256,128]{2,1,0:T(8,128)(2,1)S(1)} %shard_map.101.refs_4_.refs_2_), channel_id=1, source_target_pairs={{4,0},{8,4},{12,8},{14,12},{10,14},{6,10},{2,6},{0,2},{1,5},{5,9},... | collective-permute-start | bytes 1572872 | tf_op jit(solution)/shard_map/ppermute | solution.py:344
  71.5 9.1 %collective-permute-start.27 = (bf16[8,256,128]{2,1,0:T(8,128)(2,1)S(1)}, bf16[8,256,128]{2,1,0:T(8,128)(2,1)S(1)}, u32[]{:S(2)}, u32[]{:S(2)}) collective-permute-start(bf16[8,256,128]{2,1,0:T(8,128)(2,1)S(1)} %shard_map.103.refs_4_.refs_2_), channel_id=1, source_target_pairs={{0,1},{1,0},{2,3},{3,2},{4,5},{5,4},{6,7},{7,6},{8,9},{9,8},{10,11... | collective-permute-start | bytes 1572872 | tf_op jit(solution)/shard_map/ppermute | solution.py:347
  71.6 12.1 %collective-permute-start.26 = (bf16[8,256,128]{2,1,0:T(8,128)(2,1)S(1)}, bf16[8,256,128]{2,1,0:T(8,128)(2,1)S(1)}, u32[]{:S(2)}, u32[]{:S(2)}) collective-permute-start(bf16[8,256,128]{2,1,0:T(8,128)(2,1)S(1)} %shard_map.103.refs_4_.refs_2_), channel_id=1, source_target_pairs={{0,4},{4,8},{8,12},{12,14},{14,10},{10,6},{6,2},{2,0},{5,1},{9,5},... | collective-permute-start | bytes 1572872 | tf_op jit(solution)/shard_map/ppermute | solution.py:344
  77.7 9.8 %collective-permute-start.24 = (bf16[8,256,128]{2,1,0:T(8,128)(2,1)S(1)}, bf16[8,256,128]{2,1,0:T(8,128)(2,1)S(1)}, u32[]{:S(2)}, u32[]{:S(2)}) collective-permute-start(bf16[8,256,128]{2,1,0:T(8,128)(2,1)S(1)} %shard_map.105.refs_4_.refs_2_), channel_id=1, source_target_pairs={{4,0},{8,4},{12,8},{14,12},{10,14},{6,10},{2,6},{0,2},{1,5},{5,9},... | collective-permute-start | bytes 1572872 | tf_op jit(solution)/shard_map/ppermute | solution.py:344
  96.0 6.5 %collective-permute-start.31 = (f32[3,2,16,128]{3,2,1,0:T(8,128)S(1)}, f32[3,2,16,128]{3,2,1,0:T(8,128)S(1)}, u32[]{:S(2)}, u32[]{:S(2)}) collective-permute-start(f32[3,2,16,128]{3,2,1,0:T(8,128)S(1)} %get-tuple-element.107), channel_id=1, source_target_pairs={{0,2},{1,3},{2,0},{3,1},{4,6},{5,7},{6,4},{7,5},{8,10},{9,11},{10,... | collective-permute-start | bytes 147464 | tf_op jit(solution)/shard_map/ppermute | solution.py:201
  (14 other events, 93.9 us)
